TPU v7x, 32 devices: a whole 2x2x4 slice. The times are simulated.
32 devices in a mesh: parts: 2 (over x), lat: 16 (over z, y, core).
Axes of the slice: x: 2, y: 2, z: 4, core: 2. Of those that a mesh axis runs over, the one named last changes fastest.
Arguments:
- grid_field: float32 [368, 1440, 256], P('lat', None, 'parts'), parts along dimension 2, may hold values from -170 to 170
- norm_gain: float32 [128], P('parts'), parts along dimension 0, may hold values from 0.5 to 1.5
- filter_weight: bfloat16 [352, 2, 64, 128], P('lat', None, None, 'parts'), parts along dimension 3, may hold values from -0.5 to 0.5
Outputs:
- spectrum_out: bfloat16 [352, 352, 512], P('lat', None, 'parts'), parts along dimension 2
There are 2 independent parts, one for each index of `parts`. A program takes and returns all parts, laid end to end along the dimension named above; each array names one. Nothing has to cross between parts.
All inputs are finite; a program needn't handle non-finite values.
Results may differ from a plain program's by a relative error of at most 0.0064.
Values may be sent and summed in bfloat16 or wider, within the bound.
A program may use at most 192 MiB of HBM per device.

v0:
```python
import math

import jax
import jax.numpy as jnp
from jax import lax
from jax.sharding import PartitionSpec as P

C = 64
S = 2
DEG_DEV = 22


def legendre_table(colatitude, orders, degrees, weight_scale):
    cosine = jnp.cos(colatitude)[:, None]
    sine_rows = jnp.sin(colatitude)
    order_sq = orders * orders
    log_start = 0.5 * jnp.log((2.0 * orders + 1.0) / (4.0 * math.pi)) + 0.5 * (
        lax.lgamma(orders + 0.5) - lax.lgamma(orders + 1.0) - 0.5 * math.log(math.pi)
    )
    log_diag = log_start[None, :] + orders[None, :] * jnp.log(sine_rows)[:, None]
    start_exp = 64.0 * jnp.floor(log_diag / (64.0 * math.log(2.0)))
    start_mant = jnp.exp(log_diag - start_exp * math.log(2.0))
    weights = (weight_scale * sine_rows)[:, None]
    limit = 2.0**64
    shrink = 2.0 ** (-64)

    def recurrence(state, degree):
        previous, earlier, exponent = state
        degree_value = degree.astype(orders.dtype)
        upper_coef = jnp.sqrt(
            (4.0 * degree_value * degree_value - 1.0)
            / jnp.maximum(degree_value * degree_value - order_sq, 1.0)
        )
        below = degree_value - 1.0
        lower_coef = jnp.sqrt(
            jnp.maximum(below * below - order_sq, 0.0) / jnp.maximum(4.0 * below * below - 1.0, 1.0)
        )
        recurred = upper_coef * (cosine * previous - lower_coef * earlier)
        at_start = degree_value == orders
        current = jnp.where(at_start, start_mant, jnp.where(degree_value > orders, recurred, 0.0))
        exponent = jnp.where(at_start, start_exp, exponent)
        value = (weights * (current * jnp.exp2(exponent))).astype(jnp.bfloat16)
        large = jnp.abs(current) > limit
        current = jnp.where(large, current * shrink, current)
        kept = jnp.where(large, previous * shrink, previous)
        exponent = jnp.where(large, exponent + 64.0, exponent)
        return ((current, kept, exponent), value)

    zero_state = jnp.zeros((colatitude.shape[0], orders.shape[0]), colatitude.dtype)
    last_state, stacked = lax.scan(
        recurrence,
        (zero_state, zero_state, zero_state),
        jnp.arange(degrees, dtype=jnp.int32),
        unroll=8,
    )
    return stacked


def expand_filter(filter_weight):
    real_part = filter_weight[:, 0]
    imag_part = filter_weight[:, 1]
    from_real = jnp.stack([real_part, imag_part], axis=2)
    from_imag = jnp.stack([-imag_part, real_part], axis=2)
    return jnp.stack([from_real, from_imag], axis=1)


def apply_filter(coefficients, expanded):
    shaped = coefficients.reshape(coefficients.shape[0], coefficients.shape[1], 2, S, C)
    mixed = jnp.einsum("lmrsc,lrcqo->lmqso", shaped, expanded, preferred_element_type=jnp.float32)
    return mixed.astype(jnp.bfloat16).reshape(
        coefficients.shape[0], coefficients.shape[1], 2 * S * C
    )


def moments(grid_field, sine_own, sine_total):
    first_moment = jnp.einsum("j,jnx->x", sine_own, grid_field, precision=lax.Precision.HIGHEST)
    second_moment = jnp.einsum(
        "j,jnx->x", sine_own, grid_field * grid_field, precision=lax.Precision.HIGHEST
    )
    first_moment, second_moment = lax.psum((first_moment, second_moment), "lat")
    denominator = grid_field.shape[1] * sine_total
    average = first_moment / denominator
    second_moment = second_moment / denominator
    spread = jnp.sqrt(second_moment - average * average + 1e-05)
    return (average, spread)


def fourier_sums(fourier_table, grid_data):
    return jnp.einsum("rmn,jnx->jmrx", fourier_table, grid_data, precision=lax.Precision.HIGHEST)


def body(grid_field, norm_gain, filter_weight):
    device_index = lax.axis_index("lat")
    lat_count = lax.axis_size("lat")
    band_rows = grid_field.shape[0]
    longitudes = grid_field.shape[1]
    columns = grid_field.shape[2]
    total_lat = band_rows * lat_count
    order_count = DEG_DEV * lat_count
    all_rows = jnp.arange(total_lat, dtype=jnp.int32)
    colat_all = math.pi * (all_rows.astype(jnp.float32) + 0.5) / total_lat
    sine_total = jnp.sum(jnp.sin(colat_all))
    own_rows = device_index * band_rows + jnp.arange(band_rows, dtype=jnp.int32)
    colat_own = math.pi * (own_rows.astype(jnp.float32) + 0.5) / total_lat
    sine_own = jnp.sin(colat_own)
    order_ints = jnp.arange(order_count, dtype=jnp.int32)
    lon_ints = jnp.arange(longitudes, dtype=jnp.int32)
    phases = order_ints[:, None] * lon_ints[None, :] % longitudes
    angles = 2.0 * math.pi * phases.astype(jnp.float32) / longitudes
    fourier_table = jnp.stack([jnp.cos(angles), -jnp.sin(angles)], axis=0)
    average, spread = moments(grid_field, sine_own, sine_total)
    factor = jnp.tile(norm_gain, S) / spread
    normalized = (grid_field - average) * factor
    spectral = fourier_sums(fourier_table, normalized)
    fourier = spectral.astype(jnp.bfloat16).reshape(band_rows, order_count, 2 * columns)
    weight_scale = math.pi**1.5 / math.sqrt(total_lat * longitudes)
    expanded = expand_filter(filter_weight)
    orders = (device_index * DEG_DEV + jnp.arange(DEG_DEV, dtype=jnp.int32)).astype(jnp.float32)
    legendre = legendre_table(colat_all, orders, order_count, weight_scale)
    order_coefs = jnp.einsum(
        "ljm,jmx->lmx",
        legendre,
        lax.all_to_all(fourier, "lat", split_axis=1, concat_axis=0, tiled=True),
        preferred_element_type=jnp.float32,
    )
    coefficients = lax.all_to_all(
        order_coefs.astype(jnp.bfloat16), "lat", split_axis=0, concat_axis=1, tiled=True
    )
    return apply_filter(coefficients, expanded)


def solution(mesh):
    in_specs = (P("lat", None, "parts"), P("parts"), P("lat", None, None, "parts"))
    out_specs = P("lat", None, "parts")
    return jax.shard_map(body, mesh=mesh, in_specs=in_specs, out_specs=out_specs, check_vma=False)
```

profile of v0, /device:TPU:13, one launch (start us, length us, event | category | flops | bytes accessed | tf_op | source)
XLA Modules:
  0.0 617.7 jit_solution(4828571565384696489)
XLA Ops:
  0.7 9.8 %sine_negate_fusion = (f32[1,352,1440]{2,1,0:T(8,128)S(1)}, f32[1,352,1440]{2,1,0:T(8,128)}) fusion(), kind=kLoop, calls=%fused_computation.172 | loop fusion | flops 5068800 | bytes 4055040 | tf_op jit(solution)/shard_map/neg | solution.py:110
  10.5 7.5 %multiply_reduce_fusion.1 = (f32[23,128]{1,0:T(8,128)S(1)}, f32[23,128]{1,0:T(8,128)S(1)}) fusion(f32[23,1440,128]{2,1,0:T(8,128)} %param.5), kind=kLoop, calls=%fused_computation.155 | loop fusion | flops 12712192 | bytes 16980992 | tf_op jit(solution)/shard_map/j,jnx->x/reduce_sum | solution.py:77
  18.5 21.9 %all-reduce = (f32[128]{0:T(128)S(1)}, f32[128]{0:T(128)S(1)}) all-reduce(f32[128]{0:T(128)S(1)} %convolution_bitcast_fusion.1, f32[128]{0:T(128)S(1)} %convolution_bitcast_fusion), channel_id=1, replica_groups=mesh['parts'=2,'lat'=16] {'lat'}, use_global_device_ids=true, to_apply=%region_1.2 | all-reduce | flops 256 | bytes 2048 | tf_op jit(solution)/shard_map/psum | solution.py:80
  41.0 46.7 %convert_bitcast_fusion = bf16[23,352,2,128]{3,1,2,0:T(8,128)(2,1)S(1)} fusion(f32[1,352,1440]{2,1,0:T(8,128)S(1)} %get-tuple-element.513, f32[1,352,1440]{2,1,0:T(8,128)} %get-tuple-element.514, f32[23,1440,128]{2,1,0:T(8,128)} %param.5, f32[128]{0:T(128)S(1)} %get-tuple-element.464, f32[128]{0:T(128)S(1)} %get-tuple-element.465), kind=kOutput, calls=%fused_computation.167 | convolution fusion | flops 35825680384 | bytes 25158656 | tf_op jit(solution)/shard_map/rmn,jnx->jmrx/dot_general | solution.py:89
  87.7 5.1 copy.35
  92.8 7.6 %reshape.396 = bf16[23,352,256]{2,0,1:T(8,128)(2,1)} reshape(bf16[23,352,2,128]{3,2,0,1:T(2,128)(2,1)} %copy.35) | data formatting | bytes 8290304 | tf_op jit(solution)/shard_map/reshape | solution.py:115
  100.4 16.8 %all-to-all-start = ((bf16[23,352,256]{2,0,1:T(8,128)(2,1)}), bf16[23,352,256]{2,0,1:T(8,128)(2,1)}, u32[]{:S(2)}, u32[]{:S(2)}) async-start(bf16[23,352,256]{2,0,1:T(8,128)(2,1)} %reshape.396), calls=%async_computation | async-start | bytes 8650752 | tf_op jit(solution)/shard_map/all_to_all | solution.py:123
  117.4 342.9 %while.23 = (s32[]{:T(128)}, f32[368,22]{0,1:T(8,128)S(1)}, f32[368,22]{0,1:T(8,128)S(1)}, f32[368,22]{0,1:T(8,128)S(1)}, bf16[44,8,368,22]{2,3,1,0:T(8,128)(2,1...) while((s32[]{:T(128)}, f32[368,22]{0,1:T(8,128)S(1)}, ...), condition=%wide.region_6.7_spmd.clone.clone.clone.clone, body=%wide.region_5.6_spmd.clone.clone.clone.clone.sunk | while | flops 2134202 | bytes 2012586 | solution.py:50
  217.9 0.7 bitcast_dynamic-update-slice_fusion.2
  288.1 0.7 bitcast_dynamic-update-slice_fusion.2
  350.4 0.7 bitcast_dynamic-update-slice_fusion.2
  397.2 0.7 bitcast_dynamic-update-slice_fusion.2
  405.0 0.7 bitcast_dynamic-update-slice_fusion.2
  412.8 0.7 bitcast_dynamic-update-slice_fusion.2
  460.3 4.8 copy.24
  465.1 7.0 %all_to_all.27 = bf16[368,22,256]{2,0,1:T(8,128)(2,1)} reshape(bf16[16,23,22,256]{3,1,0,2:T(8,128)(2,1)} %copy.24) | data formatting | bytes 8290304 | tf_op jit(solution)/shard_map/all_to_all | solution.py:123
  472.1 6.3 %convert_bitcast_fusion.1 = bf16[352,22,256]{2,0,1:T(8,128)(2,1)S(1)} fusion(bf16[368,22,256]{2,0,1:T(8,128)(2,1)} %all_to_all.27, bf16[352,368,22]{1,2,0:T(8,128)(2,1)} %bitcast.140), kind=kOutput, calls=%fused_computation.168 | convolution fusion | flops 1461075968 | bytes 13809664 | tf_op jit(solution)/shard_map/ljm,jmx->lmx/dot_general | solution.py:120
  478.4 4.4 copy.26
  482.7 6.2 %all-to-all-start.1 = ((bf16[352,22,256]{2,1,0:T(8,128)(2,1)}), bf16[352,22,256]{2,1,0:T(8,128)(2,1)}, u32[]{:S(2)}, u32[]{:S(2)}) async-start(bf16[352,22,256]{2,1,0:T(8,128)(2,1)} %copy.26), calls=%async_computation.1 | async-start | bytes 8650752 | tf_op jit(solution)/shard_map/all_to_all | solution.py:126
  489.8 94.4 %all-to-all-done.1 = bf16[352,22,256]{2,1,0:T(8,128)(2,1)} async-done(((bf16[352,22,256]{2,1,0:T(8,128)(2,1)}), bf16[352,22,256]{2,1,0:T(8,128)(2,1)}, u32[]{:S(2)}, u32[]{:S(2)}) %all-to-all-start.1) | async-done | bytes 3964960 | tf_op jit(solution)/shard_map/all_to_all | solution.py:126
  584.2 4.7 copy.28
  589.0 14.4 %reshape.385 = bf16[22,352,2,2,64]{4,3,2,1,0:T(2,128)(2,1)} reshape(bf16[22,16,22,256]{3,2,1,0:T(8,128)(2,1)} %copy.28) | data formatting | bytes 7929856 | tf_op jit(solution)/shard_map/reshape | solution.py:68
  603.4 8.0 %bitcast_convert_fusion = bf16[22,2,64,352,2]{3,2,4,1,0:T(8,128)(2,1)} fusion(bf16[22,352,2,2,64,1]{4,3,2,1,0,5:T(2,128)(2,1)} %bitcast.136, bf16[22,1,64,2,64]{2,4,1,3,0:T(8,128)(2,1)S(1)} %get-tuple-element.512, bf16[22,1,64,2,64]{2,4,1,3,0:T(8,128)(2,1)S(1)} %get-tuple-element.511), kind=kOutput, calls=%fused_computation.157 | convolution fusion | flops 510935040 | bytes 8650752 | tf_op jit(solution)/shard_map/lmrsc,lrcqo->lmqso/dot_general | solution.py:69
  611.4 6.3 %copy.30 = bf16[22,352,256]{2,1,0:T(8,128)(2,1)} copy(bf16[22,352,256]{1,2,0:T(8,128)(2,1)} %bitcast.137) | data formatting | bytes 7929856 | tf_op jit(solution)/shard_map/reshape | solution.py:70
  (1338 shorter events, 115.6 us)
Async XLA Ops:
  10.5 7.9 %copy-start.1 = (f32[64]{0:T(128)S(1)}, f32[64]{0:T(128)}, u32[]{:S(2)}) copy-start(f32[64]{0:T(128)} %param.6) | copy-start | bytes 772
  100.4 359.8 %all-to-all-start = ((bf16[23,352,256]{2,0,1:T(8,128)(2,1)}), bf16[23,352,256]{2,0,1:T(8,128)(2,1)}, u32[]{:S(2)}, u32[]{:S(2)}) async-start(bf16[23,352,256]{2,0,1:T(8,128)(2,1)} %reshape.396), calls=%async_computation | async-start | bytes 8650752 | tf_op jit(solution)/shard_map/all_to_all | solution.py:123
  482.7 6.2 %copy-start = (bf16[22,2,64,64]{3,2,1,0:T(8,128)(2,1)S(1)}, bf16[22,2,64,64]{3,2,1,0:T(8,128)(2,1)}, u32[]{:S(2)}) copy-start(bf16[22,2,64,64]{3,2,1,0:T(8,128)(2,1)} %param.7) | copy-start | bytes 1081348
  482.7 101.5 %all-to-all-start.1 = ((bf16[352,22,256]{2,1,0:T(8,128)(2,1)}), bf16[352,22,256]{2,1,0:T(8,128)(2,1)}, u32[]{:S(2)}, u32[]{:S(2)}) async-start(bf16[352,22,256]{2,1,0:T(8,128)(2,1)} %copy.26), calls=%async_computation.1 | async-start | bytes 8650752 | tf_op jit(solution)/shard_map/all_to_all | solution.py:126
where the time goes:
time: 622 us; the launch traced here: 618 us
  loops' own time  225 us (36%)
  local copies, waits for them, and re-layouts  115 us (18%)
  waiting for transfers between devices  94.4 us (15%)
  other arithmetic  76 us (12%)
  matrix products  61.3 us (10%)
  starting transfers between devices  23 us (4%)
  blocking collectives  21.9 us (4%)
    another operation x1, loops' own time, legendre_table(): lax.scan(recurrence, (zero_state, zero_state, zero_state), jnp.arange(deg...  225 us
    all_to_all x1, waiting for transfers between devices, body(): lax.all_to_all(order_coefs.astype(jnp.bfloat16), 'lat', split_axis=0, con...  94.4 us
    dot_general x1, matrix products, fourier_sums(): jnp.einsum('rmn,jnx->jmrx', fourier_table, grid_data, precision=lax.Preci...  46.7 us
    while x308, other arithmetic  35.7 us
    dynamic_update_slice x44, local copies, waits for them, and re-layouts, legendre_table(): lax.scan(recurrence, (zero_state, zero_state, zero_state), jnp.arange(deg...  29.9 us
    slice x44, local copies, waits for them, and re-layouts, legendre_table(): lax.scan(recurrence, (zero_state, zero_state, zero_state), jnp.arange(deg...  26.9 us
    psum x1, blocking collectives, moments(): first_moment, second_moment = lax.psum((first_moment, second_moment), 'lat')  21.9 us
    all_to_all x1, starting transfers between devices, body(): lax.all_to_all(fourier, 'lat', split_axis=1, concat_axis=0, tiled=True)  16.8 us
  transfers between devices with their start and end apart: 2, of which 1 were waited for; matrix products, arithmetic and copies ran while one was open for 19% of the time, Pallas kernels for 0%

commit v1 on v0

v1 whole, which is shorter than its diff:
```python
import math

import jax
import jax.numpy as jnp
import numpy as np
from jax import lax
from jax.experimental import pallas as pl
from jax.experimental.pallas import tpu as pltpu
from jax.sharding import PartitionSpec as P

C = 64
S = 2
DEG_DEV = 22
ORDER_PAD = 24
BLOCK = 16
LANES = 128


def round_up(value, step):
    return -(-value // step) * step


def legendre_kernel(
    orders_ref, cosine_ref, weights_ref, mant_ref, exp_ref, out_ref, prev_ref, early_ref, grow_ref, rows_ref
):
    block = pl.program_id(0)
    width = cosine_ref.shape[1]
    kept_width = out_ref.shape[2]

    @pl.when(block == 0)
    def _():
        prev_ref[...] = jnp.zeros_like(prev_ref)
        early_ref[...] = jnp.zeros_like(early_ref)
        grow_ref[...] = jnp.zeros_like(grow_ref)

    orders = orders_ref[...]
    narrow = orders[:, :LANES]
    order_sq = narrow * narrow
    cosine = cosine_ref[...]
    weights = weights_ref[...]
    limit = 2.0**64
    shrink = 2.0 ** (-64)
    previous, earlier, exponent = prev_ref[...], early_ref[...], grow_ref[...]
    first = (block * BLOCK).astype(jnp.float32)

    def widen(value):
        return jnp.concatenate([value] * (width // LANES), axis=1)

    for step in range(BLOCK):
        degree = first + float(step)
        upper = jnp.sqrt(
            (4.0 * degree * degree - 1.0) / jnp.maximum(degree * degree - order_sq, 1.0)
        )
        below = degree - 1.0
        lower = jnp.sqrt(
            jnp.maximum(below * below - order_sq, 0.0)
            / jnp.maximum(jnp.full_like(order_sq, 4.0 * below * below - 1.0), 1.0)
        )
        recurred = widen(upper) * (cosine * previous - widen(lower) * earlier)
        at_start = orders == degree
        current = jnp.where(at_start, mant_ref[...], jnp.where(orders < degree, recurred, 0.0))
        exponent = jnp.where(at_start, exp_ref[...], exponent)
        value = weights * (current * jnp.exp2(exponent))
        for lane in range(width // LANES):
            rows_ref[lane, step * ORDER_PAD : (step + 1) * ORDER_PAD, :] = value[
                :, lane * LANES : (lane + 1) * LANES
            ]
        large = jnp.abs(current) > limit
        earlier = jnp.where(large, previous * shrink, previous)
        previous = jnp.where(large, current * shrink, current)
        exponent = jnp.where(large, exponent + 64.0, exponent)

    prev_ref[...] = previous
    early_ref[...] = earlier
    grow_ref[...] = exponent
    for order in range(DEG_DEV):
        for lane in range(0, width, LANES):
            cut = min(LANES, kept_width - lane)
            piece = rows_ref[lane // LANES, pl.ds(order, BLOCK, stride=ORDER_PAD), :]
            out_ref[order, :, lane : lane + cut] = piece[:, :cut].astype(out_ref.dtype)


def legendre_table(colatitude, first_order, degrees, weight_scale):
    rows = colatitude.shape[0]
    width = round_up(rows, LANES)
    colat = jnp.concatenate([colatitude, jnp.full((width - rows,), 0.5 * math.pi, jnp.float32)])
    orders = (first_order + jnp.arange(ORDER_PAD, dtype=jnp.int32)).astype(jnp.float32)
    sine_rows = jnp.sin(colat)
    log_start = 0.5 * jnp.log((2.0 * orders + 1.0) / (4.0 * math.pi)) + 0.5 * (
        lax.lgamma(orders + 0.5) - lax.lgamma(orders + 1.0) - 0.5 * math.log(math.pi)
    )
    log_diag = log_start[:, None] + orders[:, None] * jnp.log(sine_rows)[None, :]
    start_exp = 64.0 * jnp.floor(log_diag / (64.0 * math.log(2.0)))
    start_mant = jnp.exp(log_diag - start_exp * math.log(2.0))
    state = (ORDER_PAD, width)
    whole = pl.BlockSpec(state, lambda i: (0, 0))
    line = pl.BlockSpec((1, width), lambda i: (0, 0))
    return pl.pallas_call(
        legendre_kernel,
        grid=(degrees // BLOCK,),
        out_shape=jax.ShapeDtypeStruct((DEG_DEV, degrees, rows), jnp.bfloat16),
        in_specs=[whole, line, line, whole, whole],
        out_specs=pl.BlockSpec((DEG_DEV, BLOCK, rows), lambda i: (0, i, 0)),
        scratch_shapes=[
            pltpu.VMEM(state, jnp.float32),
            pltpu.VMEM(state, jnp.float32),
            pltpu.VMEM(state, jnp.float32),
            pltpu.VMEM((width // LANES, BLOCK * ORDER_PAD, LANES), jnp.float32),
        ],
        cost_estimate=pl.CostEstimate(
            flops=degrees * ORDER_PAD * width * 2000,
            bytes_accessed=DEG_DEV * degrees * rows * 2,
            transcendentals=degrees * ORDER_PAD * width,
        ),
        compiler_params=pltpu.CompilerParams(vmem_limit_bytes=24 * 1024 * 1024),
    )(
        jnp.broadcast_to(orders[:, None], state),
        jnp.cos(colat)[None, :],
        (weight_scale * sine_rows)[None, :],
        start_mant,
        start_exp,
    )


def expand_filter(filter_weight):
    real_part = filter_weight[:, 0]
    imag_part = filter_weight[:, 1]
    from_real = jnp.stack([real_part, imag_part], axis=1)
    from_imag = jnp.stack([-imag_part, real_part], axis=1)
    mixing = jnp.stack([from_real, from_imag], axis=1)
    same = jnp.eye(S, dtype=filter_weight.dtype)
    full = mixing.transpose(0, 1, 3, 2, 4)[:, :, None, :, :, None, :] * same[None, None, :, None, None, :, None]
    return full.reshape(filter_weight.shape[0], 2 * S * C, 2 * S * C)


def fourier_matrix(orders, longitudes):
    phases = (np.arange(orders)[:, None] * np.arange(longitudes)[None, :]) % longitudes
    angles = 2.0 * np.pi * phases / longitudes
    return np.stack([np.cos(angles), -np.sin(angles)]).astype(np.float32)


def body(grid_field, norm_gain, filter_weight):
    device_index = lax.axis_index("lat")
    lat_count = lax.axis_size("lat")
    band_rows, longitudes, columns = grid_field.shape
    total_lat = band_rows * lat_count
    order_count = DEG_DEV * lat_count
    all_rows = jnp.arange(total_lat, dtype=jnp.int32)
    colat_all = math.pi * (all_rows.astype(jnp.float32) + 0.5) / total_lat
    sine_all = jnp.sin(colat_all)
    own_rows = device_index * band_rows + jnp.arange(band_rows, dtype=jnp.int32)
    sine_own = jnp.sin(math.pi * (own_rows.astype(jnp.float32) + 0.5) / total_lat)

    first = jnp.einsum("j,jnx->x", sine_own, grid_field, precision=lax.Precision.HIGHEST)
    second = jnp.einsum(
        "j,jnx->x", sine_own, grid_field * grid_field, precision=lax.Precision.HIGHEST
    )
    band_mean = first / (longitudes * jnp.sum(sine_own))
    gathered = lax.all_gather(jnp.stack([first, second, band_mean]), "lat")
    denominator = longitudes * jnp.sum(sine_all)
    average = jnp.sum(gathered[:, 0], axis=0) / denominator
    mean_square = jnp.sum(gathered[:, 1], axis=0) / denominator
    spread = jnp.sqrt(mean_square - average * average + 1e-05)
    factor = jnp.tile(norm_gain, S) / spread

    table = jnp.asarray(fourier_matrix(order_count, longitudes))
    raw = jnp.einsum("rmn,jnx->rmjx", table, grid_field, precision=lax.Precision.HIGH)
    constant = (jnp.arange(2)[:, None] + jnp.arange(order_count)[None, :]) == 0
    shift = jnp.where(constant[:, :, None, None], longitudes * band_mean, 0.0)
    fourier = (raw - shift).astype(jnp.bfloat16)
    received = lax.all_to_all(fourier, "lat", split_axis=1, concat_axis=2, tiled=True)

    weight_scale = math.pi**1.5 / math.sqrt(total_lat * longitudes)
    legendre = legendre_table(colat_all, device_index * DEG_DEV, order_count, weight_scale)
    sums = jnp.einsum("mlj,rmjx->mlrx", legendre, received, preferred_element_type=jnp.float32)
    band_sums = jnp.sum(
        legendre[0].astype(jnp.float32).reshape(order_count, lat_count, band_rows), axis=2
    )
    level = jnp.dot(
        band_sums,
        longitudes * (gathered[:, 2] - average),
        precision=lax.Precision.HIGHEST,
    )
    here = (device_index == 0) & (jnp.arange(DEG_DEV)[:, None] + jnp.arange(2)[None, :] == 0)
    sums = (sums + jnp.where(here[:, None, :, None], level[None, :, None, :], 0.0)) * factor
    coefficients = lax.all_to_all(
        sums.astype(jnp.bfloat16).reshape(DEG_DEV, order_count, 2 * columns),
        "lat",
        split_axis=1,
        concat_axis=0,
        tiled=True,
    )
    mixed = jnp.einsum(
        "mlx,lxy->lmy",
        coefficients,
        expand_filter(filter_weight),
        preferred_element_type=jnp.float32,
    )
    return mixed.astype(jnp.bfloat16)


def solution(mesh):
    in_specs = (P("lat", None, "parts"), P("parts"), P("lat", None, None, "parts"))
    out_specs = P("lat", None, "parts")
    return jax.shard_map(body, mesh=mesh, in_specs=in_specs, out_specs=out_specs, check_vma=False)
```

time: 622 us -> 301 us (0.48)
  loops' own time: 225 us -> 0 us
  other arithmetic: 76 us -> 9.93 us
  blocking collectives: 21.9 us -> 80.5 us
  local copies, waits for them, and re-layouts: 115 us -> 64.9 us
  matrix products: 61.3 us -> 37.7 us
  waiting for transfers between devices: 94.4 us -> 78.2 us
  Pallas kernels: 0 us -> 15.5 us
  starting transfers between devices: 23 us -> 11.8 us
    another operation x1 -> x0, loops' own time: 225 us -> none  [legendre_table(): lax.scan(recurrence, (zero_state, zero_state, zero_state), jnp.arange(deg...]
    all_gather x0 -> x1, blocking collectives: none -> 80.5 us  [body(): gathered = lax.all_gather(jnp.stack([first, second, band_mean]), 'lat')]
    while x308 -> x0, other arithmetic: 35.7 us -> none
    dynamic_update_slice x44 -> x0, local copies, waits for them, and re-layouts: 29.9 us -> none  [legendre_table(): lax.scan(recurrence, (zero_state, zero_state, zero_state), jnp.arange(deg...]
    slice x45 -> x0, local copies, waits for them, and re-layouts: 26.9 us -> none  [the longest x44 26.9 us: legendre_table(): lax.scan(recurrence, (zero_state, zero_state, zero_state), jnp.arange(deg...]
    dot_general x5 -> x6, matrix products: 61.3 us -> 37.7 us  [the longest x1 25.5 us: body(): jnp.einsum('rmn,jnx->rmjx', table, grid_field, precision=lax.Precision.HIGH)]
    psum x1 -> x0, blocking collectives: 21.9 us -> none  [moments(): first_moment, second_moment = lax.psum((first_moment, second_moment), 'lat')]
    reshape x4 -> x2, local copies, waits for them, and re-layouts: 33.5 us -> 14.9 us  [body(): sums.astype(jnp.bfloat16).reshape(DEG_DEV, order_count, 2 * columns)]
  transfers between devices with their start and end apart: 2 -> 2, of which waited for: 1 -> 1; matrix products, arithmetic and copies ran while one was open for 19% -> 7% of each run, Pallas kernels for 0% -> 5%
where the time goes in v1:
time: 301 us; the launch traced here: 300 us
  blocking collectives  80.5 us (27%)
  waiting for transfers between devices  78.2 us (26%)
  local copies, waits for them, and re-layouts  64.9 us (22%)
  matrix products  37.7 us (13%)
  Pallas kernels  15.5 us (5%)
  starting transfers between devices  11.8 us (4%)
  other arithmetic  9.93 us (3%)
    all_gather x1, blocking collectives, body(): gathered = lax.all_gather(jnp.stack([first, second, band_mean]), 'lat')  80.5 us
    all_to_all x1, waiting for transfers between devices, body(): lax.all_to_all(sums.astype(jnp.bfloat16).reshape(DEG_DEV, order_count, 2...  78.1 us
    dot_general x1, matrix products, body(): jnp.einsum('rmn,jnx->rmjx', table, grid_field, precision=lax.Precision.HIGH)  25.5 us
    mul x4, local copies, waits for them, and re-layouts, expand_filter(): mixing.transpose(0, 1, 3, 2, 4)[:, :, None, :, :, None, :]  15.6 us
    pallas_call x1, Pallas kernels, legendre_table(): pl.pallas_call(legendre_kernel, grid=(degrees // BLOCK,), out_shape=jax.S...  15.5 us
    reshape x2, local copies, waits for them, and re-layouts, body(): sums.astype(jnp.bfloat16).reshape(DEG_DEV, order_count, 2 * columns)  14.9 us
    all_to_all x3, local copies, waits for them, and re-layouts, body(): lax.all_to_all(fourier, 'lat', split_axis=1, concat_axis=2, tiled=True)  13.1 us
    all_to_all x2, local copies, waits for them, and re-layouts, body(): lax.all_to_all(sums.astype(jnp.bfloat16).reshape(DEG_DEV, order_count, 2...  11.5 us
  transfers between devices with their start and end apart: 2, of which 1 were waited for; matrix products, arithmetic and copies ran while one was open for 7% of the time, Pallas kernels for 5%

profile of v1, /device:TPU:13, one launch (start us, length us, event | category | flops | bytes accessed | tf_op | source)
XLA Modules:
  0.0 299.9 jit_solution(5763369589754932248)
XLA Ops:
  0.0 0.6 fusion.33
  0.7 7.5 %multiply_reduce_fusion = (f32[23,128]{1,0:T(8,128)S(1)}, f32[23,128]{1,0:T(8,128)S(1)}) fusion(f32[23,1440,128]{2,1,0:T(8,128)} %param.4), kind=kLoop, calls=%fused_computation.2 | loop fusion | flops 12712192 | bytes 16980992 | tf_op jit(solution)/shard_map/j,jnx->x/reduce_sum | solution.py:155
  9.2 25.5 %subtract_convert_fusion = bf16[2,352,23,128]{3,1,2,0:T(8,128)(2,1)S(1)} fusion(f32[2,352,128]{2,1,0:T(8,128)S(1)} %broadcast_select_fusion, f32[2,352,1440,1]{2,1,3,0:T(8,128)} %constant.110, f32[23,1440,128]{2,1,0:T(8,128)} %param.4), kind=kOutput, calls=%fused_computation.3 | convolution fusion | flops 17911201792 | bytes 25518080 | tf_op jit(solution)/shard_map/rmn,jnx->rmjx/dot_general | solution.py:167
  34.7 5.3 %copy.24 = bf16[2,352,23,128]{3,0,2,1:T(2,128)(2,1)} copy(bf16[2,352,23,128]{3,1,2,0:T(8,128)(2,1)S(1)} %subtract_convert_fusion) | data formatting | bytes 8290304 | tf_op jit(solution)/shard_map/convert_element_type | solution.py:170
  39.9 6.7 %all-to-all-start = ((bf16[2,352,23,128]{3,0,2,1:T(2,128)(2,1)}), bf16[2,352,23,128]{3,0,2,1:T(2,128)(2,1)}, u32[]{:S(2)}, u32[]{:S(2)}) async-start(bf16[2,352,23,128]{3,0,2,1:T(2,128)(2,1)} %copy.24), calls=%async_computation | async-start | bytes 8290304 | tf_op jit(solution)/shard_map/all_to_all | solution.py:171
  46.7 0.6 sine_reduce_fusion
  48.4 15.5 %shard_map.46 = bf16[22,352,368]{2,1,0:T(8,128)(2,1)S(1)} custom-call(f32[24,384]{1,0:T(8,128)S(1)} %broadcast_in_dim.42.orders_ref, f32[1,384]{1,0:T(1,128)S(1)} %broadcast_in_dim.43.cosine_ref, f32[1,384]{1,0:T(1,128)S(1)} %broadcast_in_dim.64.weights_ref, f32[24,384]{1,0:T(8,128)S(1)} %get-tuple-element.17.mant_ref, f32[24,384]{1,0:T(8,128)S(1)} %get-tuple-element.16.exp_ref), custom_call_target="tpu_custom_call" | custom-call | flops 6488064000 | bytes 5699584 | tf_op jit(solution)/shard_map/pallas_call | solution.py:98
  63.9 2.5 copy-done
  67.0 80.5 %all-gather.1 = f32[16,3,128]{2,1,0:T(4,128)S(1)} all-gather(f32[1,3,128]{2,1,0:T(4,128)S(1)} %maximum_bitcast_fusion.2), channel_id=2, replica_groups=mesh['parts'=2,'lat'=16] {'lat'}, dimensions={0}, use_global_device_ids=true | all-gather | bytes 26112 | tf_op jit(solution)/shard_map/all_gather | solution.py:159
  147.5 0.5 fusion.16
  148.0 2.7 copy.25
  150.8 3.3 %copy.36 = bf16[2,22,16,23,128]{4,3,2,0,1:T(8,128)(2,1)} copy(bf16[2,22,16,23,128]{4,3,1,2,0:T(8,128)(2,1)S(1)} %bitcast.57) | data formatting | bytes 8290304 | tf_op jit(solution)/shard_map/all_to_all | solution.py:171
  154.0 7.1 %reshape.213 = bf16[2,22,368,128]{3,2,0,1:T(8,128)(2,1)} reshape(bf16[2,22,16,23,128]{4,3,2,0,1:T(8,128)(2,1)} %copy.36) | data formatting | bytes 8290304 | tf_op jit(solution)/shard_map/all_to_all | solution.py:171
  161.1 6.1 %multiply_convert_fusion = bf16[22,352,2,128]{3,1,2,0:T(8,128)(2,1)S(1)} fusion(f32[128]{0:T(128)S(1)} %get-tuple-element.11, f32[352,128]{1,0:T(8,128)S(1)} %fusion.16, pred[22,2]{1,0:T(8,128)(4,1)S(1)} %fusion.15, bf16[2,22,368,128]{3,2,0,1:T(8,128)(2,1)} %reshape.213, bf16[22,352,368]{2,1,0:T(8,128)(2,1)} %copy-done), kind=kOutput, calls=%fused_computation.4 | convolution fusion | flops 1467023360 | bytes 13990444 | tf_op jit(solution)/shard_map/mlj,rmjx->mlrx/dot_general | solution.py:175
  167.3 5.0 %copy.37 = bf16[22,352,2,128]{3,2,0,1:T(2,128)(2,1)} copy(bf16[22,352,2,128]{3,1,2,0:T(8,128)(2,1)S(1)} %multiply_convert_fusion) | data formatting | bytes 7929856 | tf_op jit(solution)/shard_map/reshape | solution.py:187
  172.3 9.9 %reshape.214 = bf16[22,352,256]{2,0,1:T(8,128)(2,1)} reshape(bf16[22,352,2,128]{3,2,0,1:T(2,128)(2,1)} %copy.37) | data formatting | bytes 7929856 | tf_op jit(solution)/shard_map/reshape | solution.py:187
  182.2 5.1 %all-to-all-start.1 = ((bf16[22,352,256]{2,0,1:T(8,128)(2,1)}), bf16[22,352,256]{2,0,1:T(8,128)(2,1)}, u32[]{:S(2)}, u32[]{:S(2)}) async-start(bf16[22,352,256]{2,0,1:T(8,128)(2,1)} %reshape.214), calls=%async_computation.1 | async-start | bytes 8650752 | tf_op jit(solution)/shard_map/all_to_all | solution.py:186
  187.9 1.5 copy.33
  189.4 5.0 %mul.127 = bf16[22,2,2,64,2,2,64]{6,5,4,3,2,1,0:T(2,128)(2,1)} broadcast(bf16[22,2,64,2,64]{4,3,2,1,0:T(2,128)(2,1)S(1)} %copy.33), dimensions={0,1,3,4,6} | broadcast | bytes 3604480 | tf_op jit(solution)/shard_map/mul | solution.py:132
  194.3 10.2 %mul.128 = bf16[22,256,256]{2,1,0:T(8,128)(2,1)S(1)} reshape(bf16[22,2,2,64,2,2,64]{6,5,4,3,2,1,0:T(2,128)(2,1)} %mul.127) | data formatting | bytes 5767168 | tf_op jit(solution)/shard_map/mul | solution.py:132
  205.0 78.1 %all-to-all-done.1 = bf16[22,352,256]{2,0,1:T(8,128)(2,1)} async-done(((bf16[22,352,256]{2,0,1:T(8,128)(2,1)}), bf16[22,352,256]{2,0,1:T(8,128)(2,1)}, u32[]{:S(2)}, u32[]{:S(2)}) %all-to-all-start.1) | async-done | bytes 3964960 | tf_op jit(solution)/shard_map/all_to_all | solution.py:186
  283.1 4.7 %copy.32 = bf16[16,22,22,256]{3,1,0,2:T(8,128)(2,1)} copy(bf16[16,22,22,256]{3,1,2,0:T(8,128)(2,1)} %bitcast.16) | data formatting | bytes 7929856 | tf_op jit(solution)/shard_map/all_to_all | solution.py:186
  287.8 6.8 %all_to_all.33 = bf16[352,22,256]{2,0,1:T(8,128)(2,1)} reshape(bf16[16,22,22,256]{3,1,0,2:T(8,128)(2,1)} %copy.32) | data formatting | bytes 7929856 | tf_op jit(solution)/shard_map/all_to_all | solution.py:186
  294.6 5.3 %fusion.10 = bf16[22,352,256]{2,1,0:T(8,128)(2,1)} fusion(bf16[352,22,256]{2,0,1:T(8,128)(2,1)} %all_to_all.33, bf16[22,256,256]{2,1,0:T(8,128)(2,1)S(1)} %mul.128, bf16[256,256]{1,0:T(8,128)(2,1)S(1)} %mul.130), kind=kOutput, calls=%fused_computation.9 | convolution fusion | flops 1018445824 | bytes 10944512 | tf_op jit(solution)/shard_map/mlx,lxy->lmy/dot_general | solution.py:193
  (34 shorter events, 2.4 us)
Async XLA Ops:
  39.9 6.7 %copy-start.2 = (f32[64]{0:T(128)S(1)}, f32[64]{0:T(128)}, u32[]{:S(2)}) copy-start(f32[64]{0:T(128)} %param.5) | copy-start | bytes 772
  39.9 108.1 %all-to-all-start = ((bf16[2,352,23,128]{3,0,2,1:T(2,128)(2,1)}), bf16[2,352,23,128]{3,0,2,1:T(2,128)(2,1)}, u32[]{:S(2)}, u32[]{:S(2)}) async-start(bf16[2,352,23,128]{3,0,2,1:T(2,128)(2,1)} %copy.24), calls=%async_computation | async-start | bytes 8290304 | tf_op jit(solution)/shard_map/all_to_all | solution.py:171
  63.8 2.5 copy-start
  182.2 5.1 %copy-start.1 = (bf16[22,2,64,64]{3,2,1,0:T(8,128)(2,1)S(1)}, bf16[22,2,64,64]{3,2,1,0:T(8,128)(2,1)}, u32[]{:S(2)}) copy-start(bf16[22,2,64,64]{3,2,1,0:T(8,128)(2,1)} %param.6) | copy-start | bytes 1081348
  182.2 100.9 %all-to-all-start.1 = ((bf16[22,352,256]{2,0,1:T(8,128)(2,1)}), bf16[22,352,256]{2,0,1:T(8,128)(2,1)}, u32[]{:S(2)}, u32[]{:S(2)}) async-start(bf16[22,352,256]{2,0,1:T(8,128)(2,1)} %reshape.214), calls=%async_computation.1 | async-start | bytes 8650752 | tf_op jit(solution)/shard_map/all_to_all | solution.py:186

commit v2 on v1

--- a/solution.py
+++ b/solution.py
@@ -163,39 +163,55 @@
     spread = jnp.sqrt(mean_square - average * average + 1e-05)
     factor = jnp.tile(norm_gain, S) / spread
 
-    table = jnp.asarray(fourier_matrix(order_count, longitudes))
-    raw = jnp.einsum("rmn,jnx->rmjx", table, grid_field, precision=lax.Precision.HIGH)
-    constant = (jnp.arange(2)[:, None] + jnp.arange(order_count)[None, :]) == 0
-    shift = jnp.where(constant[:, :, None, None], longitudes * band_mean, 0.0)
-    fourier = (raw - shift).astype(jnp.bfloat16)
-    received = lax.all_to_all(fourier, "lat", split_axis=1, concat_axis=2, tiled=True)
+    denominator_rows = jnp.float32(longitudes)
+    cos_table, sin_table = fourier_matrix(order_count, longitudes)
+
+    def transform(table):
+        return jnp.einsum(
+            "mn,jnx->mjx", jnp.asarray(table), grid_field, precision=lax.Precision.HIGH
+        )
+
+    def to_orders(raw):
+        return lax.all_to_all(
+            raw.astype(jnp.bfloat16), "lat", split_axis=0, concat_axis=1, tiled=True
+        )
+
+    def to_degrees(sums):
+        return lax.all_to_all(
+            sums.astype(jnp.bfloat16), "lat", split_axis=1, concat_axis=0, tiled=True
+        )
+
+    received_sin = to_orders(transform(sin_table))
+    constant = jnp.arange(order_count) == 0
+    shift = jnp.where(constant[:, None, None], denominator_rows * band_mean, 0.0)
+    received_cos = to_orders(transform(cos_table) - shift)
 
     weight_scale = math.pi**1.5 / math.sqrt(total_lat * longitudes)
     legendre = legendre_table(colat_all, device_index * DEG_DEV, order_count, weight_scale)
-    sums = jnp.einsum("mlj,rmjx->mlrx", legendre, received, preferred_element_type=jnp.float32)
+
+    def analyse(received):
+        return jnp.einsum("mlj,mjx->mlx", legendre, received, preferred_element_type=jnp.float32)
+
+    coef_sin = to_degrees(analyse(received_sin) * factor)
     band_sums = jnp.sum(
         legendre[0].astype(jnp.float32).reshape(order_count, lat_count, band_rows), axis=2
     )
     level = jnp.dot(
         band_sums,
-        longitudes * (gathered[:, 2] - average),
+        denominator_rows * (gathered[:, 2] - average),
         precision=lax.Precision.HIGHEST,
     )
-    here = (device_index == 0) & (jnp.arange(DEG_DEV)[:, None] + jnp.arange(2)[None, :] == 0)
-    sums = (sums + jnp.where(here[:, None, :, None], level[None, :, None, :], 0.0)) * factor
-    coefficients = lax.all_to_all(
-        sums.astype(jnp.bfloat16).reshape(DEG_DEV, order_count, 2 * columns),
-        "lat",
-        split_axis=1,
-        concat_axis=0,
-        tiled=True,
-    )
-    mixed = jnp.einsum(
-        "mlx,lxy->lmy",
-        coefficients,
-        expand_filter(filter_weight),
-        preferred_element_type=jnp.float32,
-    )
+    here = (device_index == 0) & (jnp.arange(DEG_DEV) == 0)
+    coef_cos = to_degrees(
+        (analyse(received_cos) + jnp.where(here[:, None, None], level[None], 0.0)) * factor
+    )
+
+    expanded = expand_filter(filter_weight)
+
+    def mix(coefficients, weights):
+        return jnp.einsum("mlx,lxy->lmy", coefficients, weights, preferred_element_type=jnp.float32)
+
+    mixed = mix(coef_sin, expanded[:, columns:]) + mix(coef_cos, expanded[:, :columns])
     return mixed.astype(jnp.bfloat16)
 
 

time: 301 us -> 288 us (0.957)
  blocking collectives: 80.5 us -> 56.7 us
  local copies, waits for them, and re-layouts: 64.9 us -> 51.6 us
  matrix products: 37.7 us -> 47.3 us
  starting transfers between devices: 11.8 us -> 21.3 us
    all_gather x1, blocking collectives: 80.5 us -> 56.7 us  [body(): gathered = lax.all_gather(jnp.stack([first, second, band_mean]), 'lat')]
    reshape x2 -> x0, local copies, waits for them, and re-layouts: 14.9 us -> none  [body(): sums.astype(jnp.bfloat16).reshape(DEG_DEV, order_count, 2 * columns)]
    dot_general x4 -> x7, matrix products: 37.4 us -> 47 us  [the longest x2 31.1 us: transform(): jnp.einsum('mn,jnx->mjx', jnp.asarray(table), grid_field, precision=lax.P...]
    all_to_all x2 -> x4, starting transfers between devices: 11.8 us -> 21.3 us  [the longest x2 11.5 us: to_orders(): lax.all_to_all(raw.astype(jnp.bfloat16), 'lat', split_axis=0, concat_axis...]
    convert_element_type x1 -> x4, local copies, waits for them, and re-layouts: 5.27 us -> 8.75 us  [the longest x2 4.43 us: to_orders(): raw.astype(jnp.bfloat16)]
    all_to_all x5 -> x8, local copies, waits for them, and re-layouts: 24.7 us -> 22 us  [the longest x4 12.3 us: to_orders(): lax.all_to_all(raw.astype(jnp.bfloat16), 'lat', split_axis=0, concat_axis...]
    all_to_all x2 -> x4, waiting for transfers between devices: 78.2 us -> 80.4 us  [the longest x2 58.6 us: to_degrees(): lax.all_to_all(sums.astype(jnp.bfloat16), 'lat', split_axis=1, concat_axi...]
  transfers between devices with their start and end apart: 2 -> 4, of which waited for: 1 -> 3; matrix products, arithmetic and copies ran while one was open for 7% -> 24% of each run, Pallas kernels for 5% -> 5%
where the time goes in v2:
time: 288 us; the launch traced here: 287 us
  waiting for transfers between devices  80.4 us (28%)
  blocking collectives  56.7 us (20%)
  local copies, waits for them, and re-layouts  51.6 us (18%)
  matrix products  47.3 us (16%)
  starting transfers between devices  21.3 us (7%)
  Pallas kernels  15.5 us (5%)
  other arithmetic  12.6 us (4%)
    all_to_all x2, waiting for transfers between devices, to_degrees(): lax.all_to_all(sums.astype(jnp.bfloat16), 'lat', split_axis=1, concat_axi...  58.6 us
    all_gather x1, blocking collectives, body(): gathered = lax.all_gather(jnp.stack([first, second, band_mean]), 'lat')  56.7 us
    dot_general x2, matrix products, transform(): jnp.einsum('mn,jnx->mjx', jnp.asarray(table), grid_field, precision=lax.P...  31.1 us
    all_to_all x2, waiting for transfers between devices, to_orders(): lax.all_to_all(raw.astype(jnp.bfloat16), 'lat', split_axis=0, concat_axis...  21.9 us
    mul x4, local copies, waits for them, and re-layouts, expand_filter(): mixing.transpose(0, 1, 3, 2, 4)[:, :, None, :, :, None, :]  15.5 us
    pallas_call x1, Pallas kernels, legendre_table(): pl.pallas_call(legendre_kernel, grid=(degrees // BLOCK,), out_shape=jax.S...  15.5 us
    all_to_all x4, local copies, waits for them, and re-layouts, to_orders(): lax.all_to_all(raw.astype(jnp.bfloat16), 'lat', split_axis=0, concat_axis...  12.3 us
    all_to_all x2, starting transfers between devices, to_orders(): lax.all_to_all(raw.astype(jnp.bfloat16), 'lat', split_axis=0, concat_axis...  11.5 us
  transfers between devices with their start and end apart: 4, of which 3 were waited for; matrix products, arithmetic and copies ran while one was open for 24% of the time, Pallas kernels for 5%

profile of v2, /device:TPU:13, one launch (start us, length us, event | category | flops | bytes accessed | tf_op | source)
XLA Modules:
  0.0 287.1 jit_solution(15121009242434055470)
XLA Ops:
  0.0 15.5 %convolution_convert_fusion = bf16[352,23,128]{2,0,1:T(8,128)(2,1)S(1)} fusion(f32[352,1440,1]{1,0,2:T(8,128)} %constant.113, f32[23,1440,128]{2,1,0:T(8,128)} %param.5), kind=kOutput, calls=%fused_computation.5 | convolution fusion | flops 8954564608 | bytes 21057536 | tf_op jit(solution)/shard_map/mn,jnx->mjx/dot_general | solution.py:170
  17.7 6.6 %all-to-all-start = ((bf16[352,23,128]{2,1,0:T(8,128)(2,1)}), bf16[352,23,128]{2,1,0:T(8,128)(2,1)S(1)}, u32[]{:S(2)}, u32[]{:S(2)}) async-start(bf16[352,23,128]{2,1,0:T(8,128)(2,1)} %copy.19), calls=%async_computation | async-start | bytes 4325376 | tf_op jit(solution)/shard_map/all_to_all | solution.py:175
  25.6 7.5 %multiply_reduce_fusion = (f32[23,128]{1,0:T(8,128)S(1)}, f32[23,128]{1,0:T(8,128)S(1)}) fusion(f32[23,1440,128]{2,1,0:T(8,128)} %param.5), kind=kLoop, calls=%fused_computation | loop fusion | flops 12712192 | bytes 16980992 | tf_op jit(solution)/shard_map/j,jnx->x/reduce_sum | solution.py:155
  33.4 15.6 %subtract_convert_fusion = bf16[352,23,128]{2,0,1:T(8,128)(2,1)S(1)} fusion(f32[352,128]{1,0:T(8,128)S(1)} %broadcast_select_fusion, f32[352,1440,1]{1,0,2:T(8,128)} %constant.114, f32[23,1440,128]{2,1,0:T(8,128)} %param.5), kind=kOutput, calls=%fused_computation.2 | convolution fusion | flops 8955600896 | bytes 21237760 | tf_op jit(solution)/shard_map/mn,jnx->mjx/dot_general | solution.py:170
  51.2 21.9 %all-to-all-done = bf16[352,23,128]{2,1,0:T(8,128)(2,1)S(1)} async-done(((bf16[352,23,128]{2,1,0:T(8,128)(2,1)}), bf16[352,23,128]{2,1,0:T(8,128)(2,1)S(1)}, u32[]{:S(2)}, u32[]{:S(2)}) %all-to-all-start) | async-done | bytes 2072608 | tf_op jit(solution)/shard_map/all_to_all | solution.py:175
  73.1 4.9 %all-to-all-start.2 = ((bf16[352,23,128]{2,1,0:T(8,128)(2,1)}), bf16[352,23,128]{2,1,0:T(8,128)(2,1)}, u32[]{:S(2)}, u32[]{:S(2)}) async-start(bf16[352,23,128]{2,1,0:T(8,128)(2,1)} %copy.25), calls=%async_computation.2 | async-start | bytes 4325376 | tf_op jit(solution)/shard_map/all_to_all | solution.py:175
  79.7 56.7 %all-gather.1 = f32[16,3,128]{2,1,0:T(4,128)S(1)} all-gather(f32[1,3,128]{2,1,0:T(4,128)S(1)} %maximum_bitcast_fusion.2), channel_id=2, replica_groups=mesh['parts'=2,'lat'=16] {'lat'}, dimensions={0}, use_global_device_ids=true | all-gather | bytes 26112 | tf_op jit(solution)/shard_map/all_gather | solution.py:159
  136.7 15.5 %shard_map.55 = bf16[22,352,368]{2,1,0:T(8,128)(2,1)S(1)} custom-call(f32[24,384]{1,0:T(8,128)S(1)} %broadcast_in_dim.59.orders_ref, f32[1,384]{1,0:T(1,128)S(1)} %broadcast_in_dim.60.cosine_ref, f32[1,384]{1,0:T(1,128)S(1)} %broadcast_in_dim.61.weights_ref, f32[24,384]{1,0:T(8,128)S(1)} %get-tuple-element.17.mant_ref, f32[24,384]{1,0:T(8,128)S(1)} %get-tuple-element.16.exp_ref), custom_call_target="tpu_custom_call" | custom-call | flops 6488064000 | bytes 5699584 | tf_op jit(solution)/shard_map/pallas_call | solution.py:98
  152.2 2.5 copy-done
  156.6 2.7 all_to_all.55
  159.3 4.4 %multiply_convert_fusion.1 = bf16[22,352,128]{2,1,0:T(8,128)(2,1)S(1)} fusion(bf16[22,352,368]{2,1,0:T(8,128)(2,1)} %copy-done, bf16[22,368,128]{2,1,0:T(8,128)(2,1)S(1)} %all_to_all.55, f32[128]{0:T(128)S(1)} %get-tuple-element.11), kind=kOutput, calls=%fused_computation.4 | convolution fusion | flops 731529216 | bytes 9755136 | tf_op jit(solution)/shard_map/mlj,mjx->mlx/dot_general | solution.py:193
  165.8 4.9 %all-to-all-start.1 = ((bf16[22,352,128]{2,0,1:T(8,128)(2,1)}), bf16[22,352,128]{2,0,1:T(8,128)(2,1)S(1)}, u32[]{:S(2)}, u32[]{:S(2)}) async-start(bf16[22,352,128]{2,0,1:T(8,128)(2,1)} %copy.21), calls=%async_computation.1 | async-start | bytes 4325376 | tf_op jit(solution)/shard_map/all_to_all | solution.py:180
  172.6 3.6 %copy.26 = bf16[22,16,23,128]{3,2,1,0:T(8,128)(2,1)} copy(bf16[22,16,23,128]{3,2,0,1:T(8,128)(2,1)} %bitcast.17) | data formatting | bytes 4145152 | tf_op jit(solution)/shard_map/all_to_all | solution.py:175
  176.2 4.1 %all_to_all.63 = bf16[22,368,128]{2,1,0:T(8,128)(2,1)} reshape(bf16[22,16,23,128]{3,2,1,0:T(8,128)(2,1)} %copy.26) | data formatting | bytes 4145152 | tf_op jit(solution)/shard_map/all_to_all | solution.py:175
  180.3 5.0 %multiply_convert_fusion = bf16[22,352,128]{2,1,0:T(8,128)(2,1)S(1)} fusion(bf16[22,352,368]{2,1,0:T(8,128)(2,1)} %copy-done, bf16[22,368,128]{2,1,0:T(8,128)(2,1)} %all_to_all.63, f32[352,128]{1,0:T(8,128)S(1)} %fusion.4, f32[128]{0:T(128)S(1)} %get-tuple-element.11, pred[22]{0:T(512)(128)(4,1)S(1)} %compare_and_fusion), kind=kOutput, calls=%fused_computation.3 | convolution fusion | flops 733511680 | bytes 9935382 | tf_op jit(solution)/shard_map/mlj,mjx->mlx/dot_general | solution.py:193
  187.5 32.1 %all-to-all-done.1 = bf16[22,352,128]{2,0,1:T(8,128)(2,1)S(1)} async-done(((bf16[22,352,128]{2,0,1:T(8,128)(2,1)}), bf16[22,352,128]{2,0,1:T(8,128)(2,1)S(1)}, u32[]{:S(2)}, u32[]{:S(2)}) %all-to-all-start.1) | async-done | bytes 1982496 | tf_op jit(solution)/shard_map/all_to_all | solution.py:180
  219.6 4.9 %all-to-all-start.3 = ((bf16[22,352,128]{2,0,1:T(8,128)(2,1)}), bf16[22,352,128]{2,0,1:T(8,128)(2,1)}, u32[]{:S(2)}, u32[]{:S(2)}) async-start(bf16[22,352,128]{2,0,1:T(8,128)(2,1)} %copy.28), calls=%async_computation.3 | async-start | bytes 4325376 | tf_op jit(solution)/shard_map/all_to_all | solution.py:180
  227.0 5.0 %mul.129 = bf16[22,2,2,64,2,2,64]{6,5,4,3,2,1,0:T(2,128)(2,1)} broadcast(bf16[22,2,64,2,64]{4,3,2,1,0:T(2,128)(2,1)S(1)} %copy.24), dimensions={0,1,3,4,6} | broadcast | bytes 3604480 | tf_op jit(solution)/shard_map/mul | solution.py:132
  231.9 10.2 %mul.130 = bf16[22,256,256]{2,1,0:T(8,128)(2,1)S(1)} reshape(bf16[22,2,2,64,2,2,64]{6,5,4,3,2,1,0:T(2,128)(2,1)} %mul.129) | data formatting | bytes 5767168 | tf_op jit(solution)/shard_map/mul | solution.py:132
  246.9 26.5 %all-to-all-done.3 = bf16[22,352,128]{2,0,1:T(8,128)(2,1)} async-done(((bf16[22,352,128]{2,0,1:T(8,128)(2,1)}), bf16[22,352,128]{2,0,1:T(8,128)(2,1)}, u32[]{:S(2)}, u32[]{:S(2)}) %all-to-all-start.3) | async-done | bytes 1982496 | tf_op jit(solution)/shard_map/all_to_all | solution.py:180
  273.4 3.6 %copy.30 = bf16[16,22,22,128]{3,1,0,2:T(8,128)(2,1)} copy(bf16[16,22,22,128]{3,1,2,0:T(8,128)(2,1)} %bitcast.21) | data formatting | bytes 3964928 | tf_op jit(solution)/shard_map/all_to_all | solution.py:180
  276.9 4.1 %all_to_all.67 = bf16[352,22,128]{2,0,1:T(8,128)(2,1)} reshape(bf16[16,22,22,128]{3,1,0,2:T(8,128)(2,1)} %copy.30) | data formatting | bytes 3964928 | tf_op jit(solution)/shard_map/all_to_all | solution.py:180
  281.0 2.9 %fusion.1 = f32[22,352,256]{2,1,0:T(8,128)S(1)} fusion(bf16[352,22,128]{2,0,1:T(8,128)(2,1)} %all_to_all.59, bf16[22,256,256]{2,1,0:T(8,128)(2,1)S(1)} %copy-done.1), kind=kOutput, calls=%fused_computation.7 | convolution fusion | flops 507510784 | bytes 11354112 | tf_op jit(solution)/shard_map/mlx,lxy->lmy/dot_general | solution.py:212
  283.9 3.1 %add_convert_fusion = bf16[22,352,256]{2,1,0:T(8,128)(2,1)} fusion(f32[22,352,256]{2,1,0:T(8,128)S(1)} %fusion.1, bf16[352,22,128]{2,0,1:T(8,128)(2,1)S(1)} %copy-done.4, bf16[22,256,256]{2,1,0:T(8,128)(2,1)S(1)} %copy-done.1), kind=kOutput, calls=%fused_computation.1 | convolution fusion | flops 511475712 | bytes 15319040 | tf_op jit(solution)/shard_map/mlx,lxy->lmy/dot_general | solution.py:212
  (54 shorter events, 22.0 us)
Async XLA Ops:
  17.7 55.4 %all-to-all-start = ((bf16[352,23,128]{2,1,0:T(8,128)(2,1)}), bf16[352,23,128]{2,1,0:T(8,128)(2,1)S(1)}, u32[]{:S(2)}, u32[]{:S(2)}) async-start(bf16[352,23,128]{2,1,0:T(8,128)(2,1)} %copy.19), calls=%async_computation | async-start | bytes 4325376 | tf_op jit(solution)/shard_map/all_to_all | solution.py:175
  51.2 28.1 %copy-start.6 = (f32[64]{0:T(128)S(1)}, f32[64]{0:T(128)}, u32[]{:S(2)}) copy-start(f32[64]{0:T(128)} %param.6) | copy-start | bytes 772
  73.1 92.7 %all-to-all-start.2 = ((bf16[352,23,128]{2,1,0:T(8,128)(2,1)}), bf16[352,23,128]{2,1,0:T(8,128)(2,1)}, u32[]{:S(2)}, u32[]{:S(2)}) async-start(bf16[352,23,128]{2,1,0:T(8,128)(2,1)} %copy.25), calls=%async_computation.2 | async-start | bytes 4325376 | tf_op jit(solution)/shard_map/all_to_all | solution.py:175
  152.1 2.5 copy-start
  165.8 53.8 %all-to-all-start.1 = ((bf16[22,352,128]{2,0,1:T(8,128)(2,1)}), bf16[22,352,128]{2,0,1:T(8,128)(2,1)S(1)}, u32[]{:S(2)}, u32[]{:S(2)}) async-start(bf16[22,352,128]{2,0,1:T(8,128)(2,1)} %copy.21), calls=%async_computation.1 | async-start | bytes 4325376 | tf_op jit(solution)/shard_map/all_to_all | solution.py:180
  187.5 37.4 %copy-start.5 = (bf16[22,2,64,64]{3,2,1,0:T(8,128)(2,1)S(1)}, bf16[22,2,64,64]{3,2,1,0:T(8,128)(2,1)}, u32[]{:S(2)}) copy-start(bf16[22,2,64,64]{3,2,1,0:T(8,128)(2,1)} %param.7) | copy-start | bytes 1081348
  219.6 4.9 %copy-start.2 = (bf16[22,352,128]{2,0,1:T(8,128)(2,1)}, bf16[22,352,128]{2,0,1:T(8,128)(2,1)S(1)}, u32[]{:S(2)}) copy-start(bf16[22,352,128]{2,0,1:T(8,128)(2,1)S(1)} %all-to-all-done.1) | copy-start | bytes 5947396
  219.6 53.8 %all-to-all-start.3 = ((bf16[22,352,128]{2,0,1:T(8,128)(2,1)}), bf16[22,352,128]{2,0,1:T(8,128)(2,1)}, u32[]{:S(2)}, u32[]{:S(2)}) async-start(bf16[22,352,128]{2,0,1:T(8,128)(2,1)} %copy.28), calls=%async_computation.3 | async-start | bytes 4325376 | tf_op jit(solution)/shard_map/all_to_all | solution.py:180
  242.1 2.6 copy-start.3
  276.9 4.1 %copy-start.1 = (bf16[22,256,256]{2,1,0:T(8,128)(2,1)S(1)}, bf16[22,256,256]{2,1,0:T(8,128)(2,1)}, u32[]{:S(2)}) copy-start(bf16[22,256,256]{2,1,0:T(8,128)(2,1)} %broadcast_multiply_fusion) | copy-start | bytes 8650756
  281.0 2.9 %copy-start.4 = (bf16[352,22,128]{2,0,1:T(8,128)(2,1)S(1)}, bf16[352,22,128]{2,0,1:T(8,128)(2,1)}, u32[]{:S(2)}) copy-start(bf16[352,22,128]{2,0,1:T(8,128)(2,1)} %all_to_all.67) | copy-start | bytes 5947396

commit v3 on v2

--- a/solution.py
+++ b/solution.py
@@ -156,43 +156,46 @@
         "j,jnx->x", sine_own, grid_field * grid_field, precision=lax.Precision.HIGHEST
     )
     band_mean = first / (longitudes * jnp.sum(sine_own))
-    gathered = lax.all_gather(jnp.stack([first, second, band_mean]), "lat")
+    denominator_rows = jnp.float32(longitudes)
+    cos_table, sin_table = fourier_matrix(order_count, longitudes)
+
+    def transform(table):
+        return jnp.einsum(
+            "mn,jnx->mjx", jnp.asarray(table), grid_field, precision=lax.Precision.HIGH
+        )
+
+    def to_orders(raw):
+        return lax.all_to_all(
+            raw.astype(jnp.bfloat16), "lat", split_axis=0, concat_axis=1, tiled=True
+        )
+
+    def to_degrees(sums):
+        return lax.all_to_all(
+            sums.astype(jnp.bfloat16), "lat", split_axis=1, concat_axis=0, tiled=True
+        )
+
+    received_sin = to_orders(transform(sin_table))
+    constant = jnp.arange(order_count) == 0
+    shift = jnp.where(constant[:, None, None], denominator_rows * band_mean, 0.0)
+    received_cos = to_orders(transform(cos_table) - shift)
+
+    weight_scale = math.pi**1.5 / math.sqrt(total_lat * longitudes)
+    legendre = legendre_table(colat_all, device_index * DEG_DEV, order_count, weight_scale)
+
+    def analyse(received):
+        return jnp.einsum("mlj,mjx->mlx", legendre, received, preferred_element_type=jnp.float32)
+
+    sums_sin = analyse(received_sin).astype(jnp.bfloat16)
+    moments, sums_sin = lax.optimization_barrier(
+        (jnp.stack([first, second, band_mean]), sums_sin)
+    )
+    gathered, sums_sin = lax.optimization_barrier((lax.all_gather(moments, "lat"), sums_sin))
     denominator = longitudes * jnp.sum(sine_all)
     average = jnp.sum(gathered[:, 0], axis=0) / denominator
     mean_square = jnp.sum(gathered[:, 1], axis=0) / denominator
     spread = jnp.sqrt(mean_square - average * average + 1e-05)
     factor = jnp.tile(norm_gain, S) / spread
-
-    denominator_rows = jnp.float32(longitudes)
-    cos_table, sin_table = fourier_matrix(order_count, longitudes)
-
-    def transform(table):
-        return jnp.einsum(
-            "mn,jnx->mjx", jnp.asarray(table), grid_field, precision=lax.Precision.HIGH
-        )
-
-    def to_orders(raw):
-        return lax.all_to_all(
-            raw.astype(jnp.bfloat16), "lat", split_axis=0, concat_axis=1, tiled=True
-        )
-
-    def to_degrees(sums):
-        return lax.all_to_all(
-            sums.astype(jnp.bfloat16), "lat", split_axis=1, concat_axis=0, tiled=True
-        )
-
-    received_sin = to_orders(transform(sin_table))
-    constant = jnp.arange(order_count) == 0
-    shift = jnp.where(constant[:, None, None], denominator_rows * band_mean, 0.0)
-    received_cos = to_orders(transform(cos_table) - shift)
-
-    weight_scale = math.pi**1.5 / math.sqrt(total_lat * longitudes)
-    legendre = legendre_table(colat_all, device_index * DEG_DEV, order_count, weight_scale)
-
-    def analyse(received):
-        return jnp.einsum("mlj,mjx->mlx", legendre, received, preferred_element_type=jnp.float32)
-
-    coef_sin = to_degrees(analyse(received_sin) * factor)
+    coef_sin = to_degrees(sums_sin)
     band_sums = jnp.sum(
         legendre[0].astype(jnp.float32).reshape(order_count, lat_count, band_rows), axis=2
     )
@@ -203,10 +206,11 @@
     )
     here = (device_index == 0) & (jnp.arange(DEG_DEV) == 0)
     coef_cos = to_degrees(
-        (analyse(received_cos) + jnp.where(here[:, None, None], level[None], 0.0)) * factor
+        analyse(received_cos) + jnp.where(here[:, None, None], level[None], 0.0)
     )
 
     expanded = expand_filter(filter_weight)
+    expanded = (expanded * jnp.tile(factor, 2)[None, :, None]).astype(jnp.bfloat16)
 
     def mix(coefficients, weights):
         return jnp.einsum("mlx,lxy->lmy", coefficients, weights, preferred_element_type=jnp.float32)

time: 288 us -> 263 us (0.913)
  blocking collectives: 56.7 us -> 28.7 us
  local copies, waits for them, and re-layouts: 51.6 us -> 54.9 us
    all_gather x1, blocking collectives: 56.7 us -> 28.7 us  [body(): lax.all_gather(moments, 'lat')]
  transfers between devices with their start and end apart: 4 -> 4, of which waited for: 3 -> 3; matrix products, arithmetic and copies ran while one was open for 24% -> 27% of each run, Pallas kernels for 5% -> 6%
where the time goes in v3:
time: 263 us; the launch traced here: 262 us
  waiting for transfers between devices  79.3 us (30%)
  local copies, waits for them, and re-layouts  54.9 us (21%)
  matrix products  48 us (18%)
  blocking collectives  28.7 us (11%)
  starting transfers between devices  21.3 us (8%)
  Pallas kernels  15.5 us (6%)
  other arithmetic  13.2 us (5%)
    all_to_all x2, waiting for transfers between devices, to_degrees(): lax.all_to_all(sums.astype(jnp.bfloat16), 'lat', split_axis=1, concat_axi...  57.3 us
    dot_general x2, matrix products, transform(): jnp.einsum('mn,jnx->mjx', jnp.asarray(table), grid_field, precision=lax.P...  31.1 us
    all_gather x1, blocking collectives, body(): lax.all_gather(moments, 'lat')  28.7 us
    all_to_all x2, waiting for transfers between devices, to_orders(): lax.all_to_all(raw.astype(jnp.bfloat16), 'lat', split_axis=0, concat_axis...  22 us
    mul x4, local copies, waits for them, and re-layouts, expand_filter(): mixing.transpose(0, 1, 3, 2, 4)[:, :, None, :, :, None, :]  15.5 us
    pallas_call x1, Pallas kernels, legendre_table(): pl.pallas_call(legendre_kernel, grid=(degrees // BLOCK,), out_shape=jax.S...  15.5 us
    all_to_all x4, local copies, waits for them, and re-layouts, to_orders(): lax.all_to_all(raw.astype(jnp.bfloat16), 'lat', split_axis=0, concat_axis...  13.7 us
    all_to_all x2, starting transfers between devices, to_orders(): lax.all_to_all(raw.astype(jnp.bfloat16), 'lat', split_axis=0, concat_axis...  11.5 us
  transfers between devices with their start and end apart: 4, of which 3 were waited for; matrix products, arithmetic and copies ran while one was open for 27% of the time, Pallas kernels for 6%

profile of v3, /device:TPU:13, one launch (start us, length us, event | category | flops | bytes accessed | tf_op | source)
XLA Modules:
  0.0 262.4 jit_solution(16609279494354056330)
XLA Ops:
  0.0 15.5 %convolution_convert_fusion = bf16[352,23,128]{2,0,1:T(8,128)(2,1)S(1)} fusion(f32[352,1440,1]{1,0,2:T(8,128)} %constant.113, f32[23,1440,128]{2,1,0:T(8,128)} %param.5), kind=kOutput, calls=%fused_computation.5 | convolution fusion | flops 8954564608 | bytes 21057536 | tf_op jit(solution)/shard_map/mn,jnx->mjx/dot_general | solution.py:163
  17.7 6.6 %all-to-all-start = ((bf16[352,23,128]{2,1,0:T(8,128)(2,1)}), bf16[352,23,128]{2,1,0:T(8,128)(2,1)S(1)}, u32[]{:S(2)}, u32[]{:S(2)}) async-start(bf16[352,23,128]{2,1,0:T(8,128)(2,1)} %copy.19), calls=%async_computation | async-start | bytes 4325376 | tf_op jit(solution)/shard_map/all_to_all | solution.py:168
  25.6 7.5 %multiply_reduce_fusion = (f32[23,128]{1,0:T(8,128)S(1)}, f32[23,128]{1,0:T(8,128)S(1)}) fusion(f32[23,1440,128]{2,1,0:T(8,128)} %param.5), kind=kLoop, calls=%fused_computation | loop fusion | flops 12712192 | bytes 16980992 | tf_op jit(solution)/shard_map/j,jnx->x/reduce_sum | solution.py:155
  33.4 15.6 %subtract_convert_fusion = bf16[352,23,128]{2,0,1:T(8,128)(2,1)S(1)} fusion(f32[352,128]{1,0:T(8,128)S(1)} %broadcast_select_fusion, f32[352,1440,1]{1,0,2:T(8,128)} %constant.114, f32[23,1440,128]{2,1,0:T(8,128)} %param.5), kind=kOutput, calls=%fused_computation.3 | convolution fusion | flops 8955600896 | bytes 21237760 | tf_op jit(solution)/shard_map/mn,jnx->mjx/dot_general | solution.py:163
  51.1 22.0 %all-to-all-done = bf16[352,23,128]{2,1,0:T(8,128)(2,1)S(1)} async-done(((bf16[352,23,128]{2,1,0:T(8,128)(2,1)}), bf16[352,23,128]{2,1,0:T(8,128)(2,1)S(1)}, u32[]{:S(2)}, u32[]{:S(2)}) %all-to-all-start) | async-done | bytes 2072608 | tf_op jit(solution)/shard_map/all_to_all | solution.py:168
  74.4 4.9 %all-to-all-start.2 = ((bf16[352,23,128]{2,1,0:T(8,128)(2,1)}), bf16[352,23,128]{2,1,0:T(8,128)(2,1)S(1)}, u32[]{:S(2)}, u32[]{:S(2)}) async-start(bf16[352,23,128]{2,1,0:T(8,128)(2,1)} %copy.25), calls=%async_computation.2 | async-start | bytes 4325376 | tf_op jit(solution)/shard_map/all_to_all | solution.py:168
  79.9 15.5 %shard_map.55 = bf16[22,352,368]{2,1,0:T(8,128)(2,1)S(1)} custom-call(f32[24,384]{1,0:T(8,128)S(1)} %broadcast_in_dim.57.orders_ref, f32[1,384]{1,0:T(1,128)S(1)} %broadcast_in_dim.58.cosine_ref, f32[1,384]{1,0:T(1,128)S(1)} %broadcast_in_dim.59.weights_ref, f32[24,384]{1,0:T(8,128)S(1)} %get-tuple-element.25.mant_ref, f32[24,384]{1,0:T(8,128)S(1)} %get-tuple-element.24.exp_ref), custom_call_target="tpu_custom_call" | custom-call | flops 6488064000 | bytes 5699584 | tf_op jit(solution)/shard_map/pallas_call | solution.py:98
  95.4 2.5 copy-done
  99.8 4.1 %all_to_all.55 = bf16[22,368,128]{2,1,0:T(8,128)(2,1)} reshape(bf16[22,16,23,128]{3,2,1,0:T(8,128)(2,1)} %copy.20) | data formatting | bytes 4145152 | tf_op jit(solution)/shard_map/all_to_all | solution.py:168
  103.9 5.0 %convolution_convert_fusion.1 = bf16[22,352,128]{2,1,0:T(8,128)(2,1)S(1)} fusion(bf16[22,352,368]{2,1,0:T(8,128)(2,1)} %copy-done, bf16[22,368,128]{2,1,0:T(8,128)(2,1)} %all_to_all.55), kind=kOutput, calls=%fused_computation.6 | convolution fusion | flops 730537984 | bytes 9754624 | tf_op jit(solution)/shard_map/mlj,mjx->mlx/dot_general | solution.py:186
  109.0 28.7 %all-gather.1 = f32[16,3,128]{2,1,0:T(4,128)S(1)} all-gather(f32[1,3,128]{2,1,0:T(4,128)S(1)} %bitcast.62), channel_id=2, replica_groups=mesh['parts'=2,'lat'=16] {'lat'}, dimensions={0}, use_global_device_ids=true | all-gather | bytes 26112 | tf_op jit(solution)/shard_map/all_gather | solution.py:192
  141.1 5.0 %all-to-all-start.1 = ((bf16[22,352,128]{2,0,1:T(8,128)(2,1)}), bf16[22,352,128]{2,0,1:T(8,128)(2,1)S(1)}, u32[]{:S(2)}, u32[]{:S(2)}) async-start(bf16[22,352,128]{2,0,1:T(8,128)(2,1)} %copy.21), calls=%async_computation.1 | async-start | bytes 4325376 | tf_op jit(solution)/shard_map/all_to_all | solution.py:173
  148.9 3.6 %copy.26 = bf16[22,16,23,128]{3,2,1,0:T(8,128)(2,1)} copy(bf16[22,16,23,128]{3,2,0,1:T(8,128)(2,1)} %bitcast.58) | data formatting | bytes 4145152 | tf_op jit(solution)/shard_map/all_to_all | solution.py:168
  152.5 4.1 %all_to_all.63 = bf16[22,368,128]{2,1,0:T(8,128)(2,1)} reshape(bf16[22,16,23,128]{3,2,1,0:T(8,128)(2,1)} %copy.26) | data formatting | bytes 4145152 | tf_op jit(solution)/shard_map/all_to_all | solution.py:168
  157.1 5.1 %add_convert_fusion.1 = bf16[22,352,128]{2,1,0:T(8,128)(2,1)S(1)} fusion(bf16[22,352,368]{2,1,0:T(8,128)(2,1)} %copy-done, bf16[22,368,128]{2,1,0:T(8,128)(2,1)} %all_to_all.63, f32[352,128]{1,0:T(8,128)S(1)} %fusion.4, pred[22]{0:T(512)(128)(4,1)S(1)} %compare_and_fusion), kind=kOutput, calls=%fused_computation.4 | convolution fusion | flops 732520448 | bytes 9934870 | tf_op jit(solution)/shard_map/mlj,mjx->mlx/dot_general | solution.py:186
  164.3 30.6 %all-to-all-done.1 = bf16[22,352,128]{2,0,1:T(8,128)(2,1)S(1)} async-done(((bf16[22,352,128]{2,0,1:T(8,128)(2,1)}), bf16[22,352,128]{2,0,1:T(8,128)(2,1)S(1)}, u32[]{:S(2)}, u32[]{:S(2)}) %all-to-all-start.1) | async-done | bytes 1982496 | tf_op jit(solution)/shard_map/all_to_all | solution.py:173
  194.9 4.9 %all-to-all-start.3 = ((bf16[22,352,128]{2,0,1:T(8,128)(2,1)}), bf16[22,352,128]{2,0,1:T(8,128)(2,1)}, u32[]{:S(2)}, u32[]{:S(2)}) async-start(bf16[22,352,128]{2,0,1:T(8,128)(2,1)} %copy.28), calls=%async_computation.3 | async-start | bytes 4325376 | tf_op jit(solution)/shard_map/all_to_all | solution.py:173
  202.3 5.0 %mul.121 = bf16[22,2,2,64,2,2,64]{6,5,4,3,2,1,0:T(2,128)(2,1)} broadcast(bf16[22,2,64,2,64]{4,3,2,1,0:T(2,128)(2,1)S(1)} %copy.24), dimensions={0,1,3,4,6} | broadcast | bytes 3604480 | tf_op jit(solution)/shard_map/mul | solution.py:132
  207.3 10.2 %mul.122 = bf16[22,256,256]{2,1,0:T(8,128)(2,1)S(1)} reshape(bf16[22,2,2,64,2,2,64]{6,5,4,3,2,1,0:T(2,128)(2,1)} %mul.121) | data formatting | bytes 5767168 | tf_op jit(solution)/shard_map/mul | solution.py:132
  222.0 26.8 %all-to-all-done.3 = bf16[22,352,128]{2,0,1:T(8,128)(2,1)} async-done(((bf16[22,352,128]{2,0,1:T(8,128)(2,1)}), bf16[22,352,128]{2,0,1:T(8,128)(2,1)}, u32[]{:S(2)}, u32[]{:S(2)}) %all-to-all-start.3) | async-done | bytes 1982496 | tf_op jit(solution)/shard_map/all_to_all | solution.py:173
  248.7 3.6 %copy.30 = bf16[16,22,22,128]{3,1,0,2:T(8,128)(2,1)} copy(bf16[16,22,22,128]{3,1,2,0:T(8,128)(2,1)} %bitcast.22) | data formatting | bytes 3964928 | tf_op jit(solution)/shard_map/all_to_all | solution.py:173
  252.3 4.1 %all_to_all.67 = bf16[352,22,128]{2,0,1:T(8,128)(2,1)} reshape(bf16[16,22,22,128]{3,1,0,2:T(8,128)(2,1)} %copy.30) | data formatting | bytes 3964928 | tf_op jit(solution)/shard_map/all_to_all | solution.py:173
  256.4 2.9 %fusion.1 = f32[22,352,256]{2,1,0:T(8,128)S(1)} fusion(bf16[352,22,128]{2,0,1:T(8,128)(2,1)} %all_to_all.59, bf16[22,256,256]{2,1,0:T(8,128)(2,1)S(1)} %copy-done.1), kind=kOutput, calls=%fused_computation.8 | convolution fusion | flops 507510784 | bytes 11354112 | tf_op jit(solution)/shard_map/mlx,lxy->lmy/dot_general | solution.py:216
  259.3 3.1 %add_convert_fusion = bf16[22,352,256]{2,1,0:T(8,128)(2,1)} fusion(f32[22,352,256]{2,1,0:T(8,128)S(1)} %fusion.1, bf16[352,22,128]{2,0,1:T(8,128)(2,1)S(1)} %copy-done.7, bf16[22,256,256]{2,1,0:T(8,128)(2,1)S(1)} %copy-done.1), kind=kOutput, calls=%fused_computation.1 | convolution fusion | flops 511475712 | bytes 15319040 | tf_op jit(solution)/shard_map/mlx,lxy->lmy/dot_general | solution.py:216
  (61 shorter events, 24.3 us)
Async XLA Ops:
  17.7 55.4 %all-to-all-start = ((bf16[352,23,128]{2,1,0:T(8,128)(2,1)}), bf16[352,23,128]{2,1,0:T(8,128)(2,1)S(1)}, u32[]{:S(2)}, u32[]{:S(2)}) async-start(bf16[352,23,128]{2,1,0:T(8,128)(2,1)} %copy.19), calls=%async_computation | async-start | bytes 4325376 | tf_op jit(solution)/shard_map/all_to_all | solution.py:168
  73.1 1.3 copy-start.5
  74.4 65.3 %all-to-all-start.2 = ((bf16[352,23,128]{2,1,0:T(8,128)(2,1)}), bf16[352,23,128]{2,1,0:T(8,128)(2,1)S(1)}, u32[]{:S(2)}, u32[]{:S(2)}) async-start(bf16[352,23,128]{2,1,0:T(8,128)(2,1)} %copy.25), calls=%async_computation.2 | async-start | bytes 4325376 | tf_op jit(solution)/shard_map/all_to_all | solution.py:168
  79.9 18.0 %copy-start.6 = (bf16[352,23,128]{2,1,0:T(8,128)(2,1)S(1)}, bf16[352,23,128]{2,1,0:T(8,128)(2,1)}, u32[]{:S(2)}) copy-start(bf16[352,23,128]{2,1,0:T(8,128)(2,1)} %copy-done.5) | copy-start | bytes 6217732
  95.3 2.5 copy-start
  139.7 7.6 %copy-start.9 = (f32[64]{0:T(128)S(1)}, f32[64]{0:T(128)}, u32[]{:S(2)}) copy-start(f32[64]{0:T(128)} %param.6) | copy-start | bytes 772
  139.8 1.3 copy-start.4
  141.1 53.8 %all-to-all-start.1 = ((bf16[22,352,128]{2,0,1:T(8,128)(2,1)}), bf16[22,352,128]{2,0,1:T(8,128)(2,1)S(1)}, u32[]{:S(2)}, u32[]{:S(2)}) async-start(bf16[22,352,128]{2,0,1:T(8,128)(2,1)} %copy.21), calls=%async_computation.1 | async-start | bytes 4325376 | tf_op jit(solution)/shard_map/all_to_all | solution.py:173
  164.3 35.9 %copy-start.8 = (bf16[22,2,64,64]{3,2,1,0:T(8,128)(2,1)S(1)}, bf16[22,2,64,64]{3,2,1,0:T(8,128)(2,1)}, u32[]{:S(2)}) copy-start(bf16[22,2,64,64]{3,2,1,0:T(8,128)(2,1)} %param.7) | copy-start | bytes 1081348
  194.9 4.9 %copy-start.2 = (bf16[22,352,128]{2,0,1:T(8,128)(2,1)}, bf16[22,352,128]{2,0,1:T(8,128)(2,1)S(1)}, u32[]{:S(2)}) copy-start(bf16[22,352,128]{2,0,1:T(8,128)(2,1)S(1)} %all-to-all-done.1) | copy-start | bytes 5947396
  194.9 53.8 %all-to-all-start.3 = ((bf16[22,352,128]{2,0,1:T(8,128)(2,1)}), bf16[22,352,128]{2,0,1:T(8,128)(2,1)}, u32[]{:S(2)}, u32[]{:S(2)}) async-start(bf16[22,352,128]{2,0,1:T(8,128)(2,1)} %copy.28), calls=%async_computation.3 | async-start | bytes 4325376 | tf_op jit(solution)/shard_map/all_to_all | solution.py:173
  217.4 2.4 copy-start.3
  252.3 4.1 %copy-start.1 = (bf16[22,256,256]{2,1,0:T(8,128)(2,1)S(1)}, bf16[22,256,256]{2,1,0:T(8,128)(2,1)}, u32[]{:S(2)}) copy-start(bf16[22,256,256]{2,1,0:T(8,128)(2,1)} %multiply_convert_fusion) | copy-start | bytes 8650756
  256.4 2.9 %copy-start.7 = (bf16[352,22,128]{2,0,1:T(8,128)(2,1)S(1)}, bf16[352,22,128]{2,0,1:T(8,128)(2,1)}, u32[]{:S(2)}) copy-start(bf16[352,22,128]{2,0,1:T(8,128)(2,1)} %all_to_all.67) | copy-start | bytes 5947396

commit v4 on v3

--- a/solution.py
+++ b/solution.py
@@ -133,6 +133,36 @@
     return full.reshape(filter_weight.shape[0], 2 * S * C, 2 * S * C)
 
 
+def mix_kernel(sin_ref, cos_ref, weight_ref, out_ref, rows_ref):
+    sources, degrees, orders, half = cos_ref.shape
+    for degree in range(degrees):
+        for source in range(sources):
+            rows = slice(source * orders, (source + 1) * orders)
+            rows_ref[degree, rows, :half] = cos_ref[source, degree].astype(jnp.float32)
+            rows_ref[degree, rows, half:] = sin_ref[source, degree].astype(jnp.float32)
+        out_ref[degree] = jnp.dot(
+            rows_ref[degree].astype(jnp.bfloat16),
+            weight_ref[degree],
+            preferred_element_type=jnp.float32,
+        ).astype(out_ref.dtype)
+
+
+def mix(coef_sin, coef_cos, weights):
+    sources, degrees, orders, half = coef_cos.shape
+    wide = weights.shape[2]
+    step = 2
+    piece = pl.BlockSpec((sources, step, orders, half), lambda i: (0, i, 0, 0))
+    return pl.pallas_call(
+        mix_kernel,
+        grid=(degrees // step,),
+        out_shape=jax.ShapeDtypeStruct((degrees, sources * orders, wide), jnp.bfloat16),
+        in_specs=[piece, piece, pl.BlockSpec((step, 2 * half, wide), lambda i: (i, 0, 0))],
+        out_specs=pl.BlockSpec((step, sources * orders, wide), lambda i: (i, 0, 0)),
+        scratch_shapes=[pltpu.VMEM((step, sources * orders, 2 * half), jnp.float32)],
+        compiler_params=pltpu.CompilerParams(vmem_limit_bytes=24 * 1024 * 1024),
+    )(coef_sin, coef_cos, weights)
+
+
 def fourier_matrix(orders, longitudes):
     phases = (np.arange(orders)[:, None] * np.arange(longitudes)[None, :]) % longitudes
     angles = 2.0 * np.pi * phases / longitudes
@@ -170,8 +200,9 @@
         )
 
     def to_degrees(sums):
+        split = sums.astype(jnp.bfloat16).transpose(1, 0, 2)
         return lax.all_to_all(
-            sums.astype(jnp.bfloat16), "lat", split_axis=1, concat_axis=0, tiled=True
+            split.reshape(lat_count, DEG_DEV, DEG_DEV, columns), "lat", split_axis=0, concat_axis=0
         )
 
     received_sin = to_orders(transform(sin_table))
@@ -212,11 +243,7 @@
     expanded = expand_filter(filter_weight)
     expanded = (expanded * jnp.tile(factor, 2)[None, :, None]).astype(jnp.bfloat16)
 
-    def mix(coefficients, weights):
-        return jnp.einsum("mlx,lxy->lmy", coefficients, weights, preferred_element_type=jnp.float32)
-
-    mixed = mix(coef_sin, expanded[:, columns:]) + mix(coef_cos, expanded[:, :columns])
-    return mixed.astype(jnp.bfloat16)
+    return mix(coef_sin, coef_cos, expanded)
 
 
 def solution(mesh):

time: 263 us -> 262 us (level)
  Pallas kernels: 15.5 us -> 24.3 us
  matrix products: 48 us -> 42 us
  local copies, waits for them, and re-layouts: 54.9 us -> 49.1 us
    all_to_all x4 -> x0, local copies, waits for them, and re-layouts: 9.79 us -> none  [to_degrees(): lax.all_to_all(sums.astype(jnp.bfloat16), 'lat', split_axis=1, concat_axi...]
    pallas_call x0 -> x1, Pallas kernels: none -> 8.86 us  [mix(): pl.pallas_call(mix_kernel, grid=(degrees // step,), out_shape=jax.ShapeDt...]
    dot_general x2 -> x0, matrix products: 6.01 us -> none  [mix(): jnp.einsum('mlx,lxy->lmy', coefficients, weights, preferred_element_type=...]
    unnamed x20 -> x16, local copies, waits for them, and re-layouts: 5.24 us -> 8.21 us
where the time goes in v4:
time: 262 us; the launch traced here: 261 us
  waiting for transfers between devices  80 us (31%)
  local copies, waits for them, and re-layouts  49.1 us (19%)
  matrix products  42 us (16%)
  blocking collectives  28.7 us (11%)
  Pallas kernels  24.3 us (9%)
  starting transfers between devices  21.3 us (8%)
  other arithmetic  13.6 us (5%)
    all_to_all x2, waiting for transfers between devices, to_degrees(): lax.all_to_all(split.reshape(lat_count, DEG_DEV, DEG_DEV, columns), 'lat'...  58.1 us
    dot_general x2, matrix products, transform(): jnp.einsum('mn,jnx->mjx', jnp.asarray(table), grid_field, precision=lax.P...  31.1 us
    all_gather x1, blocking collectives, body(): lax.all_gather(moments, 'lat')  28.7 us
    all_to_all x2, waiting for transfers between devices, to_orders(): lax.all_to_all(raw.astype(jnp.bfloat16), 'lat', split_axis=0, concat_axis...  21.9 us
    mul x4, local copies, waits for them, and re-layouts, expand_filter(): mixing.transpose(0, 1, 3, 2, 4)[:, :, None, :, :, None, :]  16.6 us
    pallas_call x1, Pallas kernels, legendre_table(): pl.pallas_call(legendre_kernel, grid=(degrees // BLOCK,), out_shape=jax.S...  15.5 us
    all_to_all x4, local copies, waits for them, and re-layouts, to_orders(): lax.all_to_all(raw.astype(jnp.bfloat16), 'lat', split_axis=0, concat_axis...  13.7 us
    all_to_all x2, starting transfers between devices, to_orders(): lax.all_to_all(raw.astype(jnp.bfloat16), 'lat', split_axis=0, concat_axis...  11.5 us
  transfers between devices with their start and end apart: 4, of which 3 were waited for; matrix products, arithmetic and copies ran while one was open for 27% of the time, Pallas kernels for 6%

profile of v4, /device:TPU:13, one launch (start us, length us, event | category | flops | bytes accessed | tf_op | source)
XLA Modules:
  0.0 260.6 jit_solution(9495714895006376737)
XLA Ops:
  0.0 15.5 %convolution_convert_fusion = bf16[352,23,128]{2,0,1:T(8,128)(2,1)S(1)} fusion(f32[352,1440,1]{1,0,2:T(8,128)} %constant.113, f32[23,1440,128]{2,1,0:T(8,128)} %param.5), kind=kOutput, calls=%fused_computation.5 | convolution fusion | flops 8954564608 | bytes 21057536 | tf_op jit(solution)/shard_map/mn,jnx->mjx/dot_general | solution.py:193
  15.5 2.2 copy.19
  17.7 6.6 %all-to-all-start = ((bf16[352,23,128]{2,1,0:T(8,128)(2,1)}), bf16[352,23,128]{2,1,0:T(8,128)(2,1)S(1)}, u32[]{:S(2)}, u32[]{:S(2)}) async-start(bf16[352,23,128]{2,1,0:T(8,128)(2,1)} %copy.19), calls=%async_computation | async-start | bytes 4325376 | tf_op jit(solution)/shard_map/all_to_all | solution.py:198
  25.6 7.5 %multiply_reduce_fusion = (f32[23,128]{1,0:T(8,128)S(1)}, f32[23,128]{1,0:T(8,128)S(1)}) fusion(f32[23,1440,128]{2,1,0:T(8,128)} %param.5), kind=kLoop, calls=%fused_computation | loop fusion | flops 12712192 | bytes 16980992 | tf_op jit(solution)/shard_map/j,jnx->x/reduce_sum | solution.py:185
  33.4 15.6 %subtract_convert_fusion = bf16[352,23,128]{2,0,1:T(8,128)(2,1)S(1)} fusion(f32[352,128]{1,0:T(8,128)S(1)} %broadcast_select_fusion, f32[352,1440,1]{1,0,2:T(8,128)} %constant.114, f32[23,1440,128]{2,1,0:T(8,128)} %param.5), kind=kOutput, calls=%fused_computation.2 | convolution fusion | flops 8955600896 | bytes 21237760 | tf_op jit(solution)/shard_map/mn,jnx->mjx/dot_general | solution.py:193
  49.0 2.2 copy.22
  51.2 21.9 %all-to-all-done = bf16[352,23,128]{2,1,0:T(8,128)(2,1)S(1)} async-done(((bf16[352,23,128]{2,1,0:T(8,128)(2,1)}), bf16[352,23,128]{2,1,0:T(8,128)(2,1)S(1)}, u32[]{:S(2)}, u32[]{:S(2)}) %all-to-all-start) | async-done | bytes 2072608 | tf_op jit(solution)/shard_map/all_to_all | solution.py:198
  74.4 4.9 %all-to-all-start.2 = ((bf16[352,23,128]{2,1,0:T(8,128)(2,1)}), bf16[352,23,128]{2,1,0:T(8,128)(2,1)S(1)}, u32[]{:S(2)}, u32[]{:S(2)}) async-start(bf16[352,23,128]{2,1,0:T(8,128)(2,1)} %copy.22), calls=%async_computation.2 | async-start | bytes 4325376 | tf_op jit(solution)/shard_map/all_to_all | solution.py:198
  79.9 15.5 %shard_map.55 = bf16[22,352,368]{2,1,0:T(8,128)(2,1)S(1)} custom-call(f32[24,384]{1,0:T(8,128)S(1)} %broadcast_in_dim.57.orders_ref, f32[1,384]{1,0:T(1,128)S(1)} %broadcast_in_dim.58.cosine_ref, f32[1,384]{1,0:T(1,128)S(1)} %broadcast_in_dim.59.weights_ref, f32[24,384]{1,0:T(8,128)S(1)} %get-tuple-element.25.mant_ref, f32[24,384]{1,0:T(8,128)S(1)} %get-tuple-element.24.exp_ref), custom_call_target="tpu_custom_call" | custom-call | flops 6488064000 | bytes 5699584 | tf_op jit(solution)/shard_map/pallas_call | solution.py:98
  95.4 2.5 copy-done.2
  99.8 4.1 %all_to_all.35 = bf16[22,368,128]{2,1,0:T(8,128)(2,1)} reshape(bf16[22,16,23,128]{3,2,1,0:T(8,128)(2,1)} %copy.20) | data formatting | bytes 4145152 | tf_op jit(solution)/shard_map/all_to_all | solution.py:198
  103.9 5.0 %convolution_convert_fusion.1 = bf16[22,352,128]{2,1,0:T(8,128)(2,1)S(1)} fusion(bf16[22,352,368]{2,1,0:T(8,128)(2,1)} %copy-done.2, bf16[22,368,128]{2,1,0:T(8,128)(2,1)} %all_to_all.35), kind=kOutput, calls=%fused_computation.6 | convolution fusion | flops 730537984 | bytes 9754624 | tf_op jit(solution)/shard_map/mlj,mjx->mlx/dot_general | solution.py:217
  109.0 28.7 %all-gather.1 = f32[16,3,128]{2,1,0:T(4,128)S(1)} all-gather(f32[1,3,128]{2,1,0:T(4,128)S(1)} %bitcast.57), channel_id=2, replica_groups=mesh['parts'=2,'lat'=16] {'lat'}, dimensions={0}, use_global_device_ids=true | all-gather | bytes 26112 | tf_op jit(solution)/shard_map/all_gather | solution.py:223
  141.1 5.0 %all-to-all-start.1 = ((bf16[16,22,22,128]{3,2,1,0:T(8,128)(2,1)}), bf16[16,22,22,128]{3,2,1,0:T(8,128)(2,1)S(1)}, u32[]{:S(2)}, u32[]{:S(2)}) async-start(bf16[16,22,22,128]{3,2,1,0:T(8,128)(2,1)} %bitcast.52), calls=%async_computation.1 | async-start | bytes 4325376 | tf_op jit(solution)/shard_map/all_to_all | solution.py:204
  149.0 3.6 %copy.23 = bf16[22,16,23,128]{3,2,1,0:T(8,128)(2,1)} copy(bf16[22,16,23,128]{3,2,0,1:T(8,128)(2,1)} %bitcast.50) | data formatting | bytes 4145152 | tf_op jit(solution)/shard_map/all_to_all | solution.py:198
  152.6 4.1 %all_to_all.40 = bf16[22,368,128]{2,1,0:T(8,128)(2,1)} reshape(bf16[22,16,23,128]{3,2,1,0:T(8,128)(2,1)} %copy.23) | data formatting | bytes 4145152 | tf_op jit(solution)/shard_map/all_to_all | solution.py:198
  157.2 5.1 %fusion = bf16[352,22,128]{2,0,1:T(8,128)(2,1)S(1)} fusion(bf16[22,352,368]{2,1,0:T(8,128)(2,1)} %copy-done.2, bf16[22,368,128]{2,1,0:T(8,128)(2,1)} %all_to_all.40, f32[352,128]{1,0:T(8,128)S(1)} %fusion.2, pred[22]{0:T(512)(128)(4,1)S(1)} %compare_and_fusion), kind=kOutput, calls=%fused_computation.4 | convolution fusion | flops 732520448 | bytes 9934870 | tf_op jit(solution)/shard_map/mlj,mjx->mlx/dot_general | solution.py:217
  164.4 30.5 %all-to-all-done.1.sin_ref = bf16[16,22,22,128]{3,2,1,0:T(8,128)(2,1)S(1)} async-done(((bf16[16,22,22,128]{3,2,1,0:T(8,128)(2,1)}), bf16[16,22,22,128]{3,2,1,0:T(8,128)(2,1)S(1)}, u32[]{:S(2)}, u32[]{:S(2)}) %all-to-all-start.1) | async-done | bytes 1982496 | tf_op jit(solution)/shard_map/all_to_all | solution.py:204
  196.3 4.9 %all-to-all-start.3 = ((bf16[16,22,22,128]{3,2,1,0:T(8,128)(2,1)}), bf16[16,22,22,128]{3,2,1,0:T(8,128)(2,1)}, u32[]{:S(2)}, u32[]{:S(2)}) async-start(bf16[16,22,22,128]{3,2,1,0:T(8,128)(2,1)} %bitcast.53), calls=%async_computation.3 | async-start | bytes 4325376 | tf_op jit(solution)/shard_map/all_to_all | solution.py:204
  203.2 5.0 %mul.126 = bf16[22,2,2,64,2,2,64]{6,5,4,3,2,1,0:T(2,128)(2,1)} broadcast(bf16[22,2,64,2,64]{4,3,2,1,0:T(2,128)(2,1)S(1)} %copy.26), dimensions={0,1,3,4,6} | broadcast | bytes 3604480 | tf_op jit(solution)/shard_map/mul | solution.py:132
  208.2 11.2 %mul.127 = bf16[22,256,256]{2,1,0:T(8,128)(2,1)} reshape(bf16[22,2,2,64,2,2,64]{6,5,4,3,2,1,0:T(2,128)(2,1)} %mul.126) | data formatting | bytes 5767168 | tf_op jit(solution)/shard_map/mul | solution.py:132
  219.9 2.6 multiply_convert_fusion.weight_ref
  222.5 27.6 %all-to-all-done.3.cos_ref = bf16[16,22,22,128]{3,2,1,0:T(8,128)(2,1)} async-done(((bf16[16,22,22,128]{3,2,1,0:T(8,128)(2,1)}), bf16[16,22,22,128]{3,2,1,0:T(8,128)(2,1)}, u32[]{:S(2)}, u32[]{:S(2)}) %all-to-all-start.3) | async-done | bytes 1982496 | tf_op jit(solution)/shard_map/all_to_all | solution.py:204
  251.7 8.9 %shard_map.56 = bf16[22,352,256]{2,1,0:T(8,128)(2,1)} custom-call(bf16[16,22,22,128]{3,2,1,0:T(8,128)(2,1)S(1)} %copy-done.1, bf16[16,22,22,128]{3,2,1,0:T(8,128)(2,1)} %all-to-all-done.3.cos_ref, bf16[22,256,256]{2,1,0:T(8,128)(2,1)S(1)} %multiply_convert_fusion.weight_ref), custom_call_target="tpu_custom_call" | custom-call | tf_op jit(solution)/shard_map/pallas_call | solution.py:155
  (52 shorter events, 18.5 us)
Async XLA Ops:
  17.7 55.4 %all-to-all-start = ((bf16[352,23,128]{2,1,0:T(8,128)(2,1)}), bf16[352,23,128]{2,1,0:T(8,128)(2,1)S(1)}, u32[]{:S(2)}, u32[]{:S(2)}) async-start(bf16[352,23,128]{2,1,0:T(8,128)(2,1)} %copy.19), calls=%async_computation | async-start | bytes 4325376 | tf_op jit(solution)/shard_map/all_to_all | solution.py:198
  73.1 1.3 copy-start.4
  74.4 65.3 %all-to-all-start.2 = ((bf16[352,23,128]{2,1,0:T(8,128)(2,1)}), bf16[352,23,128]{2,1,0:T(8,128)(2,1)S(1)}, u32[]{:S(2)}, u32[]{:S(2)}) async-start(bf16[352,23,128]{2,1,0:T(8,128)(2,1)} %copy.22), calls=%async_computation.2 | async-start | bytes 4325376 | tf_op jit(solution)/shard_map/all_to_all | solution.py:198
  79.9 18.0 %copy-start.5 = (bf16[352,23,128]{2,1,0:T(8,128)(2,1)S(1)}, bf16[352,23,128]{2,1,0:T(8,128)(2,1)}, u32[]{:S(2)}) copy-start(bf16[352,23,128]{2,1,0:T(8,128)(2,1)} %copy-done.4) | copy-start | bytes 6217732
  95.3 2.5 copy-start.2
  139.7 1.3 copy-start.3
  141.1 53.8 %all-to-all-start.1 = ((bf16[16,22,22,128]{3,2,1,0:T(8,128)(2,1)}), bf16[16,22,22,128]{3,2,1,0:T(8,128)(2,1)S(1)}, u32[]{:S(2)}, u32[]{:S(2)}) async-start(bf16[16,22,22,128]{3,2,1,0:T(8,128)(2,1)} %bitcast.52), calls=%async_computation.1 | async-start | bytes 4325376 | tf_op jit(solution)/shard_map/all_to_all | solution.py:204
  146.1 1.3 copy-start.7
  194.9 1.4 copy-start
  194.9 6.3 %copy-start.6 = (bf16[22,2,64,64]{3,2,1,0:T(8,128)(2,1)S(1)}, bf16[22,2,64,64]{3,2,1,0:T(8,128)(2,1)}, u32[]{:S(2)}) copy-start(bf16[22,2,64,64]{3,2,1,0:T(8,128)(2,1)} %param.7) | copy-start | bytes 1081348
  196.3 53.8 %all-to-all-start.3 = ((bf16[16,22,22,128]{3,2,1,0:T(8,128)(2,1)}), bf16[16,22,22,128]{3,2,1,0:T(8,128)(2,1)}, u32[]{:S(2)}, u32[]{:S(2)}) async-start(bf16[16,22,22,128]{3,2,1,0:T(8,128)(2,1)} %bitcast.53), calls=%async_computation.3 | async-start | bytes 4325376 | tf_op jit(solution)/shard_map/all_to_all | solution.py:204
  250.1 1.6 copy-start.1

commit v5 on v4

--- a/solution.py
+++ b/solution.py
@@ -200,9 +200,8 @@
         )
 
     def to_degrees(sums):
-        split = sums.astype(jnp.bfloat16).transpose(1, 0, 2)
         return lax.all_to_all(
-            split.reshape(lat_count, DEG_DEV, DEG_DEV, columns), "lat", split_axis=0, concat_axis=0
+            sums, "lat", split_axis=0, concat_axis=0
         )
 
     received_sin = to_orders(transform(sin_table))
@@ -216,7 +215,11 @@
     def analyse(received):
         return jnp.einsum("mlj,mjx->mlx", legendre, received, preferred_element_type=jnp.float32)
 
-    sums_sin = analyse(received_sin).astype(jnp.bfloat16)
+    def by_degree(sums):
+        ordered = sums.astype(jnp.bfloat16).transpose(1, 0, 2)
+        return ordered.reshape(lat_count, DEG_DEV, DEG_DEV, columns)
+
+    sums_sin = by_degree(analyse(received_sin))
     moments, sums_sin = lax.optimization_barrier(
         (jnp.stack([first, second, band_mean]), sums_sin)
     )
@@ -237,7 +240,7 @@
     )
     here = (device_index == 0) & (jnp.arange(DEG_DEV) == 0)
     coef_cos = to_degrees(
-        analyse(received_cos) + jnp.where(here[:, None, None], level[None], 0.0)
+        by_degree(analyse(received_cos) + jnp.where(here[:, None, None], level[None], 0.0))
     )
 
     expanded = expand_filter(filter_weight)

time: 262 us -> 260 us (level)
  no operation moved by 1% of the time
where the time goes in v5:
time: 260 us; the launch traced here: 258 us
  waiting for transfers between devices  80 us (31%)
  local copies, waits for them, and re-layouts  49.1 us (19%)
  matrix products  42 us (16%)
  blocking collectives  26.5 us (10%)
  Pallas kernels  24.4 us (9%)
  starting transfers between devices  21.3 us (8%)
  other arithmetic  13.6 us (5%)
    all_to_all x2, waiting for transfers between devices, to_degrees(): return lax.all_to_all(sums, 'lat', split_axis=0, concat_axis=0)  58.1 us
    dot_general x2, matrix products, transform(): jnp.einsum('mn,jnx->mjx', jnp.asarray(table), grid_field, precision=lax.P...  31.1 us
    all_gather x1, blocking collectives, body(): lax.all_gather(moments, 'lat')  26.5 us
    all_to_all x2, waiting for transfers between devices, to_orders(): lax.all_to_all(raw.astype(jnp.bfloat16), 'lat', split_axis=0, concat_axis...  21.9 us
    mul x4, local copies, waits for them, and re-layouts, expand_filter(): mixing.transpose(0, 1, 3, 2, 4)[:, :, None, :, :, None, :]  16.6 us
    pallas_call x1, Pallas kernels, legendre_table(): pl.pallas_call(legendre_kernel, grid=(degrees // BLOCK,), out_shape=jax.S...  15.5 us
    all_to_all x4, local copies, waits for them, and re-layouts, to_orders(): lax.all_to_all(raw.astype(jnp.bfloat16), 'lat', split_axis=0, concat_axis...  13.7 us
    all_to_all x2, starting transfers between devices, to_orders(): lax.all_to_all(raw.astype(jnp.bfloat16), 'lat', split_axis=0, concat_axis...  11.5 us
  transfers between devices with their start and end apart: 4, of which 3 were waited for; matrix products, arithmetic and copies ran while one was open for 27% of the time, Pallas kernels for 6%

profile of v5, /device:TPU:13, one launch (start us, length us, event | category | flops | bytes accessed | tf_op | source)
XLA Modules:
  0.0 258.5 jit_solution(3099734840731700369)
XLA Ops:
  0.0 15.5 %convolution_convert_fusion = bf16[352,23,128]{2,0,1:T(8,128)(2,1)S(1)} fusion(f32[352,1440,1]{1,0,2:T(8,128)} %constant.113, f32[23,1440,128]{2,1,0:T(8,128)} %param.5), kind=kOutput, calls=%fused_computation.6 | convolution fusion | flops 8954564608 | bytes 21057536 | tf_op jit(solution)/shard_map/mn,jnx->mjx/dot_general | solution.py:193
  15.5 2.2 copy.19
  17.7 6.6 %all-to-all-start = ((bf16[352,23,128]{2,1,0:T(8,128)(2,1)}), bf16[352,23,128]{2,1,0:T(8,128)(2,1)S(1)}, u32[]{:S(2)}, u32[]{:S(2)}) async-start(bf16[352,23,128]{2,1,0:T(8,128)(2,1)} %copy.19), calls=%async_computation | async-start | bytes 4325376 | tf_op jit(solution)/shard_map/all_to_all | solution.py:198
  25.6 7.5 %multiply_reduce_fusion = (f32[23,128]{1,0:T(8,128)S(1)}, f32[23,128]{1,0:T(8,128)S(1)}) fusion(f32[23,1440,128]{2,1,0:T(8,128)} %param.5), kind=kLoop, calls=%fused_computation | loop fusion | flops 12712192 | bytes 16980992 | tf_op jit(solution)/shard_map/j,jnx->x/reduce_sum | solution.py:185
  33.4 15.6 %subtract_convert_fusion = bf16[352,23,128]{2,0,1:T(8,128)(2,1)S(1)} fusion(f32[352,128]{1,0:T(8,128)S(1)} %broadcast_select_fusion, f32[352,1440,1]{1,0,2:T(8,128)} %constant.114, f32[23,1440,128]{2,1,0:T(8,128)} %param.5), kind=kOutput, calls=%fused_computation.2 | convolution fusion | flops 8955600896 | bytes 21237760 | tf_op jit(solution)/shard_map/mn,jnx->mjx/dot_general | solution.py:193
  49.0 2.2 copy.22
  51.2 21.9 %all-to-all-done = bf16[352,23,128]{2,1,0:T(8,128)(2,1)S(1)} async-done(((bf16[352,23,128]{2,1,0:T(8,128)(2,1)}), bf16[352,23,128]{2,1,0:T(8,128)(2,1)S(1)}, u32[]{:S(2)}, u32[]{:S(2)}) %all-to-all-start) | async-done | bytes 2072608 | tf_op jit(solution)/shard_map/all_to_all | solution.py:198
  74.4 4.9 %all-to-all-start.2 = ((bf16[352,23,128]{2,1,0:T(8,128)(2,1)}), bf16[352,23,128]{2,1,0:T(8,128)(2,1)S(1)}, u32[]{:S(2)}, u32[]{:S(2)}) async-start(bf16[352,23,128]{2,1,0:T(8,128)(2,1)} %copy.22), calls=%async_computation.2 | async-start | bytes 4325376 | tf_op jit(solution)/shard_map/all_to_all | solution.py:198
  79.9 15.5 %shard_map.55 = bf16[22,352,368]{2,1,0:T(8,128)(2,1)S(1)} custom-call(f32[24,384]{1,0:T(8,128)S(1)} %broadcast_in_dim.57.orders_ref, f32[1,384]{1,0:T(1,128)S(1)} %broadcast_in_dim.58.cosine_ref, f32[1,384]{1,0:T(1,128)S(1)} %broadcast_in_dim.59.weights_ref, f32[24,384]{1,0:T(8,128)S(1)} %get-tuple-element.25.mant_ref, f32[24,384]{1,0:T(8,128)S(1)} %get-tuple-element.24.exp_ref), custom_call_target="tpu_custom_call" | custom-call | flops 6488064000 | bytes 5699584 | tf_op jit(solution)/shard_map/pallas_call | solution.py:98
  95.4 2.5 copy-done.2
  99.8 4.1 %all_to_all.35 = bf16[22,368,128]{2,1,0:T(8,128)(2,1)} reshape(bf16[22,16,23,128]{3,2,1,0:T(8,128)(2,1)} %copy.20) | data formatting | bytes 4145152 | tf_op jit(solution)/shard_map/all_to_all | solution.py:198
  103.9 5.0 %convert_bitcast_fusion = bf16[352,22,128]{2,0,1:T(8,128)(2,1)S(1)} fusion(bf16[22,352,368]{2,1,0:T(8,128)(2,1)} %copy-done.2, bf16[22,368,128]{2,1,0:T(8,128)(2,1)} %all_to_all.35), kind=kOutput, calls=%fused_computation.5 | convolution fusion | flops 730537984 | bytes 9754624 | tf_op jit(solution)/shard_map/mlj,mjx->mlx/dot_general | solution.py:216
  111.1 26.5 %all-gather.1 = f32[16,3,128]{2,1,0:T(4,128)S(1)} all-gather(f32[1,3,128]{2,1,0:T(4,128)S(1)} %bitcast.57), channel_id=2, replica_groups=mesh['parts'=2,'lat'=16] {'lat'}, dimensions={0}, use_global_device_ids=true | all-gather | bytes 26112 | tf_op jit(solution)/shard_map/all_gather | solution.py:226
  138.9 5.0 %all-to-all-start.1 = ((bf16[16,22,22,128]{3,2,1,0:T(8,128)(2,1)}), bf16[16,22,22,128]{3,2,1,0:T(8,128)(2,1)S(1)}, u32[]{:S(2)}, u32[]{:S(2)}) async-start(bf16[16,22,22,128]{3,2,1,0:T(8,128)(2,1)} %bitcast.53), calls=%async_computation.1 | async-start | bytes 4325376 | tf_op jit(solution)/shard_map/all_to_all | solution.py:203
  146.8 3.6 %copy.23 = bf16[22,16,23,128]{3,2,1,0:T(8,128)(2,1)} copy(bf16[22,16,23,128]{3,2,0,1:T(8,128)(2,1)} %bitcast.51) | data formatting | bytes 4145152 | tf_op jit(solution)/shard_map/all_to_all | solution.py:198
  150.5 4.1 %all_to_all.40 = bf16[22,368,128]{2,1,0:T(8,128)(2,1)} reshape(bf16[22,16,23,128]{3,2,1,0:T(8,128)(2,1)} %copy.23) | data formatting | bytes 4145152 | tf_op jit(solution)/shard_map/all_to_all | solution.py:198
  155.0 5.1 %fusion = bf16[352,22,128]{2,0,1:T(8,128)(2,1)S(1)} fusion(bf16[22,352,368]{2,1,0:T(8,128)(2,1)} %copy-done.2, bf16[22,368,128]{2,1,0:T(8,128)(2,1)} %all_to_all.40, f32[352,128]{1,0:T(8,128)S(1)} %fusion.2, pred[22]{0:T(512)(128)(4,1)S(1)} %compare_and_fusion), kind=kOutput, calls=%fused_computation.4 | convolution fusion | flops 732520448 | bytes 9934870 | tf_op jit(solution)/shard_map/mlj,mjx->mlx/dot_general | solution.py:216
  162.2 30.5 %all-to-all-done.1.sin_ref = bf16[16,22,22,128]{3,2,1,0:T(8,128)(2,1)S(1)} async-done(((bf16[16,22,22,128]{3,2,1,0:T(8,128)(2,1)}), bf16[16,22,22,128]{3,2,1,0:T(8,128)(2,1)S(1)}, u32[]{:S(2)}, u32[]{:S(2)}) %all-to-all-start.1) | async-done | bytes 1982496 | tf_op jit(solution)/shard_map/all_to_all | solution.py:203
  194.1 4.9 %all-to-all-start.3 = ((bf16[16,22,22,128]{3,2,1,0:T(8,128)(2,1)}), bf16[16,22,22,128]{3,2,1,0:T(8,128)(2,1)}, u32[]{:S(2)}, u32[]{:S(2)}) async-start(bf16[16,22,22,128]{3,2,1,0:T(8,128)(2,1)} %bitcast.54), calls=%async_computation.3 | async-start | bytes 4325376 | tf_op jit(solution)/shard_map/all_to_all | solution.py:203
  201.1 5.0 %mul.126 = bf16[22,2,2,64,2,2,64]{6,5,4,3,2,1,0:T(2,128)(2,1)} broadcast(bf16[22,2,64,2,64]{4,3,2,1,0:T(2,128)(2,1)S(1)} %copy.26), dimensions={0,1,3,4,6} | broadcast | bytes 3604480 | tf_op jit(solution)/shard_map/mul | solution.py:132
  206.1 11.2 %mul.127 = bf16[22,256,256]{2,1,0:T(8,128)(2,1)} reshape(bf16[22,2,2,64,2,2,64]{6,5,4,3,2,1,0:T(2,128)(2,1)} %mul.126) | data formatting | bytes 5767168 | tf_op jit(solution)/shard_map/mul | solution.py:132
  217.8 2.6 multiply_convert_fusion.weight_ref
  220.4 27.6 %all-to-all-done.3.cos_ref = bf16[16,22,22,128]{3,2,1,0:T(8,128)(2,1)} async-done(((bf16[16,22,22,128]{3,2,1,0:T(8,128)(2,1)}), bf16[16,22,22,128]{3,2,1,0:T(8,128)(2,1)}, u32[]{:S(2)}, u32[]{:S(2)}) %all-to-all-start.3) | async-done | bytes 1982496 | tf_op jit(solution)/shard_map/all_to_all | solution.py:203
  249.6 8.9 %shard_map.56 = bf16[22,352,256]{2,1,0:T(8,128)(2,1)} custom-call(bf16[16,22,22,128]{3,2,1,0:T(8,128)(2,1)S(1)} %copy-done.1, bf16[16,22,22,128]{3,2,1,0:T(8,128)(2,1)} %all-to-all-done.3.cos_ref, bf16[22,256,256]{2,1,0:T(8,128)(2,1)S(1)} %multiply_convert_fusion.weight_ref), custom_call_target="tpu_custom_call" | custom-call | tf_op jit(solution)/shard_map/pallas_call | solution.py:155
  (52 shorter events, 18.5 us)
Async XLA Ops:
  17.7 55.4 %all-to-all-start = ((bf16[352,23,128]{2,1,0:T(8,128)(2,1)}), bf16[352,23,128]{2,1,0:T(8,128)(2,1)S(1)}, u32[]{:S(2)}, u32[]{:S(2)}) async-start(bf16[352,23,128]{2,1,0:T(8,128)(2,1)} %copy.19), calls=%async_computation | async-start | bytes 4325376 | tf_op jit(solution)/shard_map/all_to_all | solution.py:198
  73.1 1.3 copy-start.4
  74.4 63.2 %all-to-all-start.2 = ((bf16[352,23,128]{2,1,0:T(8,128)(2,1)}), bf16[352,23,128]{2,1,0:T(8,128)(2,1)S(1)}, u32[]{:S(2)}, u32[]{:S(2)}) async-start(bf16[352,23,128]{2,1,0:T(8,128)(2,1)} %copy.22), calls=%async_computation.2 | async-start | bytes 4325376 | tf_op jit(solution)/shard_map/all_to_all | solution.py:198
  79.9 18.0 %copy-start.5 = (bf16[352,23,128]{2,1,0:T(8,128)(2,1)S(1)}, bf16[352,23,128]{2,1,0:T(8,128)(2,1)}, u32[]{:S(2)}) copy-start(bf16[352,23,128]{2,1,0:T(8,128)(2,1)} %copy-done.4) | copy-start | bytes 6217732
  95.4 2.5 copy-start.2
  137.6 1.3 copy-start.3
  138.9 53.8 %all-to-all-start.1 = ((bf16[16,22,22,128]{3,2,1,0:T(8,128)(2,1)}), bf16[16,22,22,128]{3,2,1,0:T(8,128)(2,1)S(1)}, u32[]{:S(2)}, u32[]{:S(2)}) async-start(bf16[16,22,22,128]{3,2,1,0:T(8,128)(2,1)} %bitcast.53), calls=%async_computation.1 | async-start | bytes 4325376 | tf_op jit(solution)/shard_map/all_to_all | solution.py:203
  143.9 1.3 copy-start.7
  192.7 1.4 copy-start
  192.7 6.3 %copy-start.6 = (bf16[22,2,64,64]{3,2,1,0:T(8,128)(2,1)S(1)}, bf16[22,2,64,64]{3,2,1,0:T(8,128)(2,1)}, u32[]{:S(2)}) copy-start(bf16[22,2,64,64]{3,2,1,0:T(8,128)(2,1)} %param.7) | copy-start | bytes 1081348
  194.1 53.8 %all-to-all-start.3 = ((bf16[16,22,22,128]{3,2,1,0:T(8,128)(2,1)}), bf16[16,22,22,128]{3,2,1,0:T(8,128)(2,1)}, u32[]{:S(2)}, u32[]{:S(2)}) async-start(bf16[16,22,22,128]{3,2,1,0:T(8,128)(2,1)} %bitcast.54), calls=%async_computation.3 | async-start | bytes 4325376 | tf_op jit(solution)/shard_map/all_to_all | solution.py:203
  248.0 1.6 copy-start.1
